TPU v7x, 256 devices: a whole 4x4x8 slice. The times are simulated.
256 devices in a mesh: tm: 64 (over y, z, core), obs: 4 (over x).
Axes of the slice: x: 4, y: 4, z: 8, core: 2. Of those that a mesh axis runs over, the one named last changes fastest.
Arguments:
- weights: bfloat16 [64, 16384, 128], P('tm', 'obs'), may hold values from -0.0546875 to 0.0546875
- tile_of: int32 [64, 16384], P('tm', 'obs'), may hold values from 0 to 31
- obs_prec: float32 [64, 16384], P('tm', 'obs'), may hold values from 0.01 to 0.4
- obs_value: float32 [64, 16384], P('tm', 'obs'), may hold values from -6 to 6
- node_kappa: float32 [4096], P('obs'), may hold values from 0.5 to 4
- rate: float32 [64, 32], P('tm', 'obs'), may hold values from 0.94 to 0.99
Outputs:
- post_mean: float32 [64, 4096], P('tm', 'obs')
Inputs may be any that keep to these rules, and one draw needn't show every extreme that they name: `tile_of`: every entry names one of the 32 tiles.
All inputs are finite; a program needn't handle non-finite values.
Results may differ from a plain program's by a relative error of at most 0.00035.
Values may be sent and summed in bfloat16 or wider, within the bound.
A program may use at most 64 MiB of HBM per device.

v0:
```python
import math

import jax
import jax.numpy as jnp
from jax import lax
from jax.sharding import PartitionSpec as P


def passed_along(array, axis, by):
    peers = lax.axis_size(axis)
    pairs = [(i, i + by) for i in range(peers) if 0 <= i + by < peers]
    return lax.ppermute(array, axis, pairs)


def spatial_prior(kappa):
    kappa_tiles = kappa.reshape(-1, 128)
    position = jnp.arange(128)
    degree = jnp.where((position == 0) | (position == 127), 1.0, 2.0).astype(jnp.float32)
    identity = jnp.eye(128, dtype=jnp.float32)
    neighbour = (jnp.abs(position[:, None] - position[None, :]) == 1).astype(jnp.float32)
    return (kappa_tiles + degree)[:, :, None] * identity - neighbour


def pairwise(left, right):
    return jnp.einsum("kab,kac->kbc", left, right, precision=lax.Precision.HIGHEST)


def lower_solve(factor, target):
    return jax.scipy.linalg.solve_triangular(factor, target, lower=True)


def flipped(matrix):
    return jnp.swapaxes(matrix, 1, 2)


def tile_terms(rows, scaled, labels, weighted, count):
    total_rows = rows.shape[0]
    block = math.gcd(total_rows, max(8192 // count, 1))
    columns = jnp.arange(count, dtype=jnp.int32)

    def add_block(step, total):
        offset = step * block
        part_rows = lax.dynamic_slice_in_dim(rows, offset, block, 0)
        part_scaled = lax.dynamic_slice_in_dim(scaled, offset, block, 0)
        part_labels = lax.dynamic_slice_in_dim(labels, offset, block, 0)
        part_weighted = lax.dynamic_slice_in_dim(weighted, offset, block, 0)
        match = part_labels[:, None] == columns[None, :]
        left = (match.astype(jnp.bfloat16)[:, :, None] * part_scaled[:, None, :]).reshape(
            block, count * 128
        )
        matrix = lax.dot_general(
            left, part_rows, (((0,), (0,)), ((), ())), preferred_element_type=jnp.float32
        )
        vector = lax.dot_general(
            match.astype(jnp.float32) * part_weighted[:, None],
            part_rows.astype(jnp.float32),
            (((0,), (0,)), ((), ())),
            precision=lax.Precision.HIGHEST,
        )
        return total + jnp.concatenate(
            [matrix.reshape(count, 128, 128), vector[:, None, :]], axis=1
        )

    return lax.fori_loop(
        0, total_rows // block, add_block, jnp.zeros((count, 129, 128), jnp.float32)
    )


def on_device(weights, tile_of, obs_prec, obs_value, node_kappa, rate):
    owned = node_kappa.shape[0] // 128
    widened = weights[0].astype(jnp.float32)
    scaled = (obs_prec[0][:, None] * widened).astype(jnp.bfloat16)
    weighted = obs_prec[0] * obs_value[0]
    totals = lax.psum_scatter(
        tile_terms(weights[0], scaled, tile_of[0], weighted, owned * lax.axis_size("obs")),
        "obs",
        scatter_dimension=0,
        tiled=True,
    )
    gram = totals[:, :128, :]
    right_side = totals[:, 128, :]
    prior = spatial_prior(node_kappa)
    devices = lax.axis_size("tm")
    position = lax.axis_index("tm")
    rate_here = rate[0]
    rate_after = passed_along(rate, "tm", -1)[0]
    leading = jnp.where(position == 0, 1.0 - rate_here * rate_here, jnp.ones_like(rate_here))
    couple_here = jnp.where(position == 0, jnp.zeros_like(rate_here), rate_here)
    diagonal_block = (leading + rate_after * rate_after)[:, None, None] * prior + gram
    below = -couple_here[:, None, None] * prior
    above = -rate_after[:, None, None] * prior
    identity = jnp.broadcast_to(jnp.eye(128, dtype=jnp.float32), (owned, 128, 128))
    stride = 1
    while stride < devices:
        factor = jnp.linalg.cholesky(diagonal_block)
        left_factor, left_below, left_side = passed_along((factor, below, right_side), "tm", stride)
        right_factor, right_above, right_far = passed_along(
            (factor, above, right_side), "tm", -stride
        )
        left_factor = jnp.where(position >= stride, left_factor, identity)
        right_factor = jnp.where(position < devices - stride, right_factor, identity)
        upper = lower_solve(left_factor, flipped(below))
        upper_couple = lower_solve(left_factor, left_below)
        upper_side = lower_solve(left_factor, left_side[:, :, None])
        lower_part = lower_solve(right_factor, flipped(above))
        lower_couple = lower_solve(right_factor, right_above)
        lower_side = lower_solve(right_factor, right_far[:, :, None])
        diagonal_block = diagonal_block - pairwise(upper, upper) - pairwise(lower_part, lower_part)
        below = -pairwise(upper, upper_couple)
        above = -pairwise(lower_part, lower_couple)
        right_side = (
            right_side
            - pairwise(upper, upper_side)[:, :, 0]
            - pairwise(lower_part, lower_side)[:, :, 0]
        )
        stride = stride * 2
    factor = jnp.linalg.cholesky(diagonal_block)
    forward = lower_solve(factor, right_side[:, :, None])
    solution = jax.scipy.linalg.solve_triangular(factor, forward, lower=True, trans=1)[:, :, 0]
    return solution.reshape(1, owned * 128)


def solution(mesh):
    placed = (
        P("tm", "obs", None),
        P("tm", "obs"),
        P("tm", "obs"),
        P("tm", "obs"),
        P("obs"),
        P("tm", "obs"),
    )
    return jax.shard_map(
        on_device, mesh=mesh, in_specs=placed, out_specs=P("tm", "obs"), check_vma=False
    )
```

profile of v0, /device:TPU:1, one launch (start us, length us, event | category | flops | bytes accessed | tf_op | source)
XLA Modules:
  0.0 2098.3 jit_solution(14808771497491319466)
XLA Ops:
  9.1 67.6 %while.14 = (s32[]{:T(128)}, f32[32,129,128]{2,1,0:T(8,128)S(1)}, s32[4096]{0:T(1024)}, bf16[4096,128]{1,0:T(8,128)(2,1)S(1)}, bf16[4096,128]{1,0:T(8,128)(2,1)}...) while((s32[]{:T(128)}, f32[32,129,128]{2,1,0:T(8,128)S(1)}, ...), condition=%wide.region_1.0_spmd.clone, body=%wide.region_0.0_spmd.clone.sunk | while | flops 283684864 | bytes 8953017 | solution.py:64
  78.0 5.1 collective-permute-start
  84.2 31.1 %reduce-scatter.2.cloned.1.call-done = f32[8,129,128]{2,1,0:T(8,128)} async-done(((f32[32,129,128]{2,1,0:T(8,128)}), f32[8,129,128]{2,1,0:T(8,128)}) %reduce-scatter.2.cloned.1.call-update) | async-done | bytes 528400 | tf_op jit(solution)/shard_map/reduce_scatter | solution.py:74
  115.3 2.3 fusion.97
  118.1 93.8 %custom-call.54 = f32[8,128,128]{2,1,0:T(8,128)S(1)} custom-call(f32[8,128,128]{2,1,0:T(8,128)S(1)} %copy.98), custom_call_target="Cholesky" | custom-call | tf_op jit(solution)/shard_map/jit(cholesky)/cholesky | solution.py:95
  212.2 2.5 collective-permute-start.2
  214.7 3.1 collective-permute-start.1
  218.6 1.9 collective-permute-start.24
  220.5 3.6 collective-permute-start.23
  224.2 1.9 collective-permute-start.4
  226.1 3.5 collective-permute-start.6
  230.5 78.6 %custom-call.55 = f32[8,1,128,128]{2,3,1,0:T(8,128)S(1)} custom-call(f32[8,1,128,128]{3,2,1,0:T(8,128)S(1)} %get-tuple-element.193), custom_call_target="InvertDiagBlocksLowerTriangular" | custom-call | tf_op jit(solution)/shard_map/jit(_solve_triangular)/vmap()/triangular_solve | solution.py:29
  311.7 79.4 %custom-call.56 = f32[8,1,128,128]{2,3,1,0:T(8,128)S(1)} custom-call(f32[8,1,128,128]{3,2,1,0:T(8,128)} %get-tuple-element.194), custom_call_target="InvertDiagBlocksLowerTriangular" | custom-call | tf_op jit(solution)/shard_map/jit(_solve_triangular)/vmap()/triangular_solve | solution.py:29
  395.2 4.5 collective-permute-start.25
  403.8 94.6 %custom-call.57 = f32[8,128,128]{2,1,0:T(8,128)S(1)} custom-call(f32[8,128,128]{2,1,0:T(8,128)} %copy.106), custom_call_target="Cholesky" | custom-call | tf_op jit(solution)/shard_map/jit(cholesky)/cholesky | solution.py:95
  500.0 4.0 collective-permute-start.3
  504.1 2.0 fusion.88
  507.2 5.2 collective-permute-start.8
  512.4 2.0 fusion.83
  517.9 78.6 %custom-call.59 = f32[8,1,128,128]{2,3,1,0:T(8,128)S(1)} custom-call(f32[8,1,128,128]{3,2,1,0:T(8,128)S(1)} %get-tuple-element.191), custom_call_target="InvertDiagBlocksLowerTriangular" | custom-call | tf_op jit(solution)/shard_map/jit(_solve_triangular)/vmap()/triangular_solve | solution.py:29
  596.5 78.6 %custom-call.61 = f32[8,1,128,128]{2,3,1,0:T(8,128)S(1)} custom-call(f32[8,1,128,128]{3,2,1,0:T(8,128)S(1)} %get-tuple-element.192), custom_call_target="InvertDiagBlocksLowerTriangular" | custom-call | tf_op jit(solution)/shard_map/jit(_solve_triangular)/vmap()/triangular_solve | solution.py:29
  676.1 2.0 fusion.69
  682.7 7.6 collective-permute-start.27
  692.4 1.9 fusion.68
  694.3 2.0 copy.120
  696.4 95.2 %custom-call.62 = f32[8,128,128]{2,1,0:T(8,128)} custom-call(f32[8,128,128]{2,1,0:T(8,128)} %copy.120), custom_call_target="Cholesky" | custom-call | tf_op jit(solution)/shard_map/jit(cholesky)/cholesky | solution.py:95
  795.3 6.1 collective-permute-start.7
  801.4 2.0 fusion.78
  804.5 6.2 collective-permute-start.12
  810.8 2.0 fusion.72
  814.7 7.2 collective-permute-done.9
  823.6 78.6 %custom-call.64 = f32[8,1,128,128]{2,3,1,0:T(8,128)S(1)} custom-call(f32[8,1,128,128]{3,2,1,0:T(8,128)S(1)} %get-tuple-element.189), custom_call_target="InvertDiagBlocksLowerTriangular" | custom-call | tf_op jit(solution)/shard_map/jit(_solve_triangular)/vmap()/triangular_solve | solution.py:29
  905.6 78.6 %custom-call.66 = f32[8,1,128,128]{2,3,1,0:T(8,128)S(1)} custom-call(f32[8,1,128,128]{3,2,1,0:T(8,128)S(1)} %get-tuple-element.190), custom_call_target="InvertDiagBlocksLowerTriangular" | custom-call | tf_op jit(solution)/shard_map/jit(_solve_triangular)/vmap()/triangular_solve | solution.py:29
  984.2 2.1 fusion.56
  989.3 10.8 collective-permute-start.29
  1004.1 2.0 copy.134
  1006.1 95.2 %custom-call.67 = f32[8,128,128]{2,1,0:T(8,128)} custom-call(f32[8,128,128]{2,1,0:T(8,128)} %copy.134), custom_call_target="Cholesky" | custom-call | tf_op jit(solution)/shard_map/jit(cholesky)/cholesky | solution.py:95
  1105.0 8.8 collective-permute-start.11
  1113.9 2.0 fusion.65
  1117.0 8.9 collective-permute-start.16
  1125.9 2.0 fusion.59
  1131.4 78.6 %custom-call.69 = f32[8,1,128,128]{2,3,1,0:T(8,128)S(1)} custom-call(f32[8,1,128,128]{3,2,1,0:T(8,128)S(1)} %get-tuple-element.187), custom_call_target="InvertDiagBlocksLowerTriangular" | custom-call | tf_op jit(solution)/shard_map/jit(_solve_triangular)/vmap()/triangular_solve | solution.py:29
  1213.4 78.6 %custom-call.71 = f32[8,1,128,128]{2,3,1,0:T(8,128)S(1)} custom-call(f32[8,1,128,128]{3,2,1,0:T(8,128)S(1)} %get-tuple-element.188), custom_call_target="InvertDiagBlocksLowerTriangular" | custom-call | tf_op jit(solution)/shard_map/jit(_solve_triangular)/vmap()/triangular_solve | solution.py:29
  1292.0 2.1 fusion.43
  1297.1 23.4 %collective-permute-start.31 = (f32[8,128]{1,0:T(8,128)S(1)}, f32[8,128]{1,0:T(8,128)S(1)}, u32[]{:S(2)}, u32[]{:S(2)}) collective-permute-start(f32[8,128]{1,0:T(8,128)S(1)} %subtract_subtract_fusion.2), channel_id=1, source_target_pairs={{0,64},{4,68},{8,72},{12,76},{16,80},{20,84},{24,88},{28,92},{32,9... | collective-permute-start | bytes 12296 | tf_op jit(solution)/shard_map/ppermute | solution.py:12
  1324.5 2.0 copy.148
  1326.5 95.2 %custom-call.72 = f32[8,128,128]{2,1,0:T(8,128)} custom-call(f32[8,128,128]{2,1,0:T(8,128)} %copy.148), custom_call_target="Cholesky" | custom-call | tf_op jit(solution)/shard_map/jit(cholesky)/cholesky | solution.py:95
  1425.5 24.0 %collective-permute-start.15 = (f32[8,128,128]{2,1,0:T(8,128)S(1)}, f32[8,128,128]{2,1,0:T(8,128)S(1)}, u32[]{:S(2)}, u32[]{:S(2)}) collective-permute-start(f32[8,128,128]{2,1,0:T(8,128)S(1)} %select_select_fusion.2), channel_id=1, source_target_pairs={{0,64},{4,68},{8,72},{12,76},{16,80},{20,84},{24,88},{28,92},{32,9... | collective-permute-start | bytes 1572872 | tf_op jit(solution)/shard_map/ppermute | solution.py:12
  1449.4 2.0 fusion.52
  1452.5 4.1 collective-permute-start.20
  1456.7 2.0 fusion.46
  1462.1 78.6 %custom-call.74 = f32[8,1,128,128]{2,3,1,0:T(8,128)S(1)} custom-call(f32[8,1,128,128]{3,2,1,0:T(8,128)S(1)} %get-tuple-element.185), custom_call_target="InvertDiagBlocksLowerTriangular" | custom-call | tf_op jit(solution)/shard_map/jit(_solve_triangular)/vmap()/triangular_solve | solution.py:29
  1544.1 78.6 %custom-call.76 = f32[8,1,128,128]{2,3,1,0:T(8,128)S(1)} custom-call(f32[8,1,128,128]{3,2,1,0:T(8,128)S(1)} %get-tuple-element.186), custom_call_target="InvertDiagBlocksLowerTriangular" | custom-call | tf_op jit(solution)/shard_map/jit(_solve_triangular)/vmap()/triangular_solve | solution.py:29
  1622.7 2.1 fusion.30
  1627.8 5.7 collective-permute-start.33
  1637.4 2.0 copy.162
  1639.5 95.2 %custom-call.77 = f32[8,128,128]{2,1,0:T(8,128)} custom-call(f32[8,128,128]{2,1,0:T(8,128)} %copy.162), custom_call_target="Cholesky" | custom-call | tf_op jit(solution)/shard_map/jit(cholesky)/cholesky | solution.py:95
  1738.4 5.6 collective-permute-start.19
  1744.0 2.0 fusion.39
  1747.1 2.0 fusion.33
  1751.1 79.8 %custom-call.79 = f32[8,1,128,128]{2,3,1,0:T(8,128)S(1)} custom-call(f32[8,1,128,128]{3,2,1,0:T(8,128)} %get-tuple-element.183), custom_call_target="InvertDiagBlocksLowerTriangular" | custom-call | tf_op jit(solution)/shard_map/jit(_solve_triangular)/vmap()/triangular_solve | solution.py:29
  1834.1 78.6 %custom-call.81 = f32[8,1,128,128]{2,3,1,0:T(8,128)S(1)} custom-call(f32[8,1,128,128]{3,2,1,0:T(8,128)S(1)} %get-tuple-element.184), custom_call_target="InvertDiagBlocksLowerTriangular" | custom-call | tf_op jit(solution)/shard_map/jit(_solve_triangular)/vmap()/triangular_solve | solution.py:29
  1916.3 94.0 %custom-call.82 = f32[8,128,128]{2,1,0:T(8,128)S(1)} custom-call(f32[8,128,128]{2,1,0:T(8,128)S(1)} %copy.172), custom_call_target="Cholesky" | custom-call | tf_op jit(solution)/shard_map/jit(cholesky)/cholesky | solution.py:117
  2010.6 78.6 %custom-call.13 = f32[8,1,128,128]{2,3,1,0:T(8,128)S(1)} custom-call(f32[8,1,128,128]{3,2,1,0:T(8,128)S(1)} %fusion.93), custom_call_target="InvertDiagBlocksLowerTriangular" | custom-call | tf_op jit(solution)/shard_map/jit(_solve_triangular)/vmap()/triangular_solve | solution.py:119
  (306 shorter events, 169.3 us)
Async XLA Ops:
  6.5 108.8 %reduce-scatter.2.cloned.1.call-start = ((), (), s32[]{:S(2)}) async-start(), calls=%async_computation.1 | async-start | bytes 2785280 | tf_op jit(solution)/shard_map/reduce_scatter | solution.py:74
  76.6 1.4 copy-start
  76.6 1.4 copy-start.5
  76.6 6.6 copy-start.4
  78.0 6.2 collective-permute-start
  212.2 13.9 collective-permute-start.2
  214.7 14.9 collective-permute-start.1
  218.6 174.2 %collective-permute-start.24 = (f32[8,128]{1,0:T(8,128)S(1)}, f32[8,128]{1,0:T(8,128)S(1)}, u32[]{:S(2)}, u32[]{:S(2)}) collective-permute-start(f32[8,128]{1,0:T(8,128)S(1)} %bitcast.584), channel_id=1, source_target_pairs={{4,0},{8,4},{12,8},{16,12},{20,16},{24,20},{28,24},{32,28},{36,32}... | collective-permute-start | bytes 12296 | tf_op jit(solution)/shard_map/ppermute | solution.py:12
  220.5 88.6 %collective-permute-start.23 = (f32[8,128]{1,0:T(8,128)S(1)}, f32[8,128]{1,0:T(8,128)S(1)}, u32[]{:S(2)}, u32[]{:S(2)}) collective-permute-start(f32[8,128]{1,0:T(8,128)S(1)} %bitcast.585), channel_id=1, source_target_pairs={{0,4},{4,8},{8,12},{12,16},{16,20},{20,24},{24,28},{28,32},{32,36}... | collective-permute-start | bytes 12296 | tf_op jit(solution)/shard_map/ppermute | solution.py:12
  224.2 275.9 %collective-permute-start.4 = (f32[8,128,128]{2,1,0:T(8,128)}, f32[8,128,128]{2,1,0:T(8,128)}, u32[]{:S(2)}, u32[]{:S(2)}) collective-permute-start(f32[8,128,128]{2,1,0:T(8,128)} %get-tuple-element.180), channel_id=1, source_target_pairs={{0,4},{4,8},{8,12},{12,16},{16,20},{20,24},{24,28},{28,32},{32,36}... | collective-permute-start | bytes 1572872 | tf_op jit(solution)/shard_map/ppermute | solution.py:12
  226.1 281.1 %collective-permute-start.6 = (f32[8,128,128]{2,1,0:T(8,128)}, f32[8,128,128]{2,1,0:T(8,128)}, u32[]{:S(2)}, u32[]{:S(2)}) collective-permute-start(f32[8,128,128]{2,1,0:T(8,128)} %get-tuple-element.181), channel_id=1, source_target_pairs={{4,0},{8,4},{12,8},{16,12},{20,16},{24,20},{28,24},{32,28},{36,32}... | collective-permute-start | bytes 1572872 | tf_op jit(solution)/shard_map/ppermute | solution.py:12
  393.9 284.8 %collective-permute-start.26 = (f32[8,128]{1,0:T(8,128)S(1)}, f32[8,128]{1,0:T(8,128)S(1)}, u32[]{:S(2)}, u32[]{:S(2)}) collective-permute-start(f32[8,128]{1,0:T(8,128)S(1)} %subtract_subtract_fusion.5), channel_id=1, source_target_pairs={{8,0},{12,4},{16,8},{20,12},{24,16},{28,20},{32,24},{36,28},{40,32... | collective-permute-start | bytes 12296 | tf_op jit(solution)/shard_map/ppermute | solution.py:12
  395.2 283.0 %collective-permute-start.25 = (f32[8,128]{1,0:T(8,128)S(1)}, f32[8,128]{1,0:T(8,128)S(1)}, u32[]{:S(2)}, u32[]{:S(2)}) collective-permute-start(f32[8,128]{1,0:T(8,128)S(1)} %subtract_subtract_fusion.5), channel_id=1, source_target_pairs={{0,8},{4,12},{8,16},{12,20},{16,24},{20,28},{24,32},{28,36},{32,40... | collective-permute-start | bytes 12296 | tf_op jit(solution)/shard_map/ppermute | solution.py:12
  498.7 17.6 collective-permute-start.5
  500.0 17.7 collective-permute-start.3
  507.2 288.1 %collective-permute-start.8 = (f32[8,128,128]{2,1,0:T(8,128)S(1)}, f32[8,128,128]{2,1,0:T(8,128)}, u32[]{:S(2)}, u32[]{:S(2)}) collective-permute-start(f32[8,128,128]{2,1,0:T(8,128)S(1)} %convolution_negate_fusion.9), channel_id=1, source_target_pairs={{0,8},{4,12},{8,16},{12,20},{16,24},{20,28},{24,32},{28,36},{32,40... | collective-permute-start | bytes 1572872 | tf_op jit(solution)/shard_map/ppermute | solution.py:12
  516.3 288.2 %collective-permute-start.10 = (f32[8,128,128]{2,1,0:T(8,128)}, f32[8,128,128]{2,1,0:T(8,128)}, u32[]{:S(2)}, u32[]{:S(2)}) collective-permute-start(f32[8,128,128]{2,1,0:T(8,128)} %convolution_negate_fusion.8), channel_id=1, source_target_pairs={{8,0},{12,4},{16,8},{20,12},{24,16},{28,20},{32,24},{36,28},{40,32... | collective-permute-start | bytes 1572872 | tf_op jit(solution)/shard_map/ppermute | solution.py:12
  681.4 305.5 %collective-permute-start.28 = (f32[8,128]{1,0:T(8,128)S(1)}, f32[8,128]{1,0:T(8,128)S(1)}, u32[]{:S(2)}, u32[]{:S(2)}) collective-permute-start(f32[8,128]{1,0:T(8,128)S(1)} %subtract_subtract_fusion.4), channel_id=1, source_target_pairs={{16,0},{20,4},{24,8},{28,12},{32,16},{36,20},{40,24},{44,28},{48,3... | collective-permute-start | bytes 12296 | tf_op jit(solution)/shard_map/ppermute | solution.py:12
  682.7 222.3 %collective-permute-start.27 = (f32[8,128]{1,0:T(8,128)S(1)}, f32[8,128]{1,0:T(8,128)S(1)}, u32[]{:S(2)}, u32[]{:S(2)}) collective-permute-start(f32[8,128]{1,0:T(8,128)S(1)} %subtract_subtract_fusion.4), channel_id=1, source_target_pairs={{0,16},{4,20},{8,24},{12,28},{16,32},{20,36},{24,40},{28,44},{32,4... | collective-permute-start | bytes 12296 | tf_op jit(solution)/shard_map/ppermute | solution.py:12
  794.0 27.8 %collective-permute-start.9 = (f32[8,128,128]{2,1,0:T(8,128)S(1)}, f32[8,128,128]{2,1,0:T(8,128)S(1)}, u32[]{:S(2)}, u32[]{:S(2)}) collective-permute-start(f32[8,128,128]{2,1,0:T(8,128)S(1)} %select_select_fusion.4), channel_id=1, source_target_pairs={{16,0},{20,4},{24,8},{28,12},{32,16},{36,20},{40,24},{44,28},{48,3... | collective-permute-start | bytes 1572872 | tf_op jit(solution)/shard_map/ppermute | solution.py:12
  795.3 28.2 %collective-permute-start.7 = (f32[8,128,128]{2,1,0:T(8,128)S(1)}, f32[8,128,128]{2,1,0:T(8,128)S(1)}, u32[]{:S(2)}, u32[]{:S(2)}) collective-permute-start(f32[8,128,128]{2,1,0:T(8,128)S(1)} %select_select_fusion.4), channel_id=1, source_target_pairs={{0,16},{4,20},{8,24},{12,28},{16,32},{20,36},{24,40},{28,44},{32,4... | collective-permute-start | bytes 1572872 | tf_op jit(solution)/shard_map/ppermute | solution.py:12
  804.5 300.5 %collective-permute-start.12 = (f32[8,128,128]{2,1,0:T(8,128)S(1)}, f32[8,128,128]{2,1,0:T(8,128)}, u32[]{:S(2)}, u32[]{:S(2)}) collective-permute-start(f32[8,128,128]{2,1,0:T(8,128)S(1)} %convolution_negate_fusion.7), channel_id=1, source_target_pairs={{0,16},{4,20},{8,24},{12,28},{16,32},{20,36},{24,40},{28,44},{32,4... | collective-permute-start | bytes 1572872 | tf_op jit(solution)/shard_map/ppermute | solution.py:12
  821.8 295.2 %collective-permute-start.14 = (f32[8,128,128]{2,1,0:T(8,128)}, f32[8,128,128]{2,1,0:T(8,128)}, u32[]{:S(2)}, u32[]{:S(2)}) collective-permute-start(f32[8,128,128]{2,1,0:T(8,128)} %convolution_negate_fusion.6), channel_id=1, source_target_pairs={{16,0},{20,4},{24,8},{28,12},{32,16},{36,20},{40,24},{44,28},{48,3... | collective-permute-start | bytes 1572872 | tf_op jit(solution)/shard_map/ppermute | solution.py:12
  984.2 15.9 copy-start.1
  988.0 306.7 %collective-permute-start.30 = (f32[8,128]{1,0:T(8,128)S(1)}, f32[8,128]{1,0:T(8,128)S(1)}, u32[]{:S(2)}, u32[]{:S(2)}) collective-permute-start(f32[8,128]{1,0:T(8,128)S(1)} %subtract_subtract_fusion.3), channel_id=1, source_target_pairs={{32,0},{36,4},{40,8},{44,12},{48,16},{52,20},{56,24},{60,28},{64,3... | collective-permute-start | bytes 12296 | tf_op jit(solution)/shard_map/ppermute | solution.py:12
  989.3 223.6 %collective-permute-start.29 = (f32[8,128]{1,0:T(8,128)S(1)}, f32[8,128]{1,0:T(8,128)S(1)}, u32[]{:S(2)}, u32[]{:S(2)}) collective-permute-start(f32[8,128]{1,0:T(8,128)S(1)} %subtract_subtract_fusion.3), channel_id=1, source_target_pairs={{0,32},{4,36},{8,40},{12,44},{16,48},{20,52},{24,56},{28,60},{32,6... | collective-permute-start | bytes 12296 | tf_op jit(solution)/shard_map/ppermute | solution.py:12
  1103.7 26.1 %collective-permute-start.13 = (f32[8,128,128]{2,1,0:T(8,128)S(1)}, f32[8,128,128]{2,1,0:T(8,128)S(1)}, u32[]{:S(2)}, u32[]{:S(2)}) collective-permute-start(f32[8,128,128]{2,1,0:T(8,128)S(1)} %select_select_fusion.3), channel_id=1, source_target_pairs={{32,0},{36,4},{40,8},{44,12},{48,16},{52,20},{56,24},{60,28},{64,3... | collective-permute-start | bytes 1572872 | tf_op jit(solution)/shard_map/ppermute | solution.py:12
  1105.0 26.3 %collective-permute-start.11 = (f32[8,128,128]{2,1,0:T(8,128)S(1)}, f32[8,128,128]{2,1,0:T(8,128)S(1)}, u32[]{:S(2)}, u32[]{:S(2)}) collective-permute-start(f32[8,128,128]{2,1,0:T(8,128)S(1)} %select_select_fusion.3), channel_id=1, source_target_pairs={{0,32},{4,36},{8,40},{12,44},{16,48},{20,52},{24,56},{28,60},{32,6... | collective-permute-start | bytes 1572872 | tf_op jit(solution)/shard_map/ppermute | solution.py:12
  1117.0 308.5 %collective-permute-start.16 = (f32[8,128,128]{2,1,0:T(8,128)S(1)}, f32[8,128,128]{2,1,0:T(8,128)}, u32[]{:S(2)}, u32[]{:S(2)}) collective-permute-start(f32[8,128,128]{2,1,0:T(8,128)S(1)} %convolution_negate_fusion.5), channel_id=1, source_target_pairs={{0,32},{4,36},{8,40},{12,44},{16,48},{20,52},{24,56},{28,60},{32,6... | collective-permute-start | bytes 1572872 | tf_op jit(solution)/shard_map/ppermute | solution.py:12
  1129.8 322.7 %collective-permute-start.18 = (f32[8,128,128]{2,1,0:T(8,128)}, f32[8,128,128]{2,1,0:T(8,128)}, u32[]{:S(2)}, u32[]{:S(2)}) collective-permute-start(f32[8,128,128]{2,1,0:T(8,128)} %convolution_negate_fusion.4), channel_id=1, source_target_pairs={{32,0},{36,4},{40,8},{44,12},{48,16},{52,20},{56,24},{60,28},{64,3... | collective-permute-start | bytes 1572872 | tf_op jit(solution)/shard_map/ppermute | solution.py:12
  1292.0 28.5 %copy-start.2 = (f32[8,128,128]{2,1,0:T(8,128)S(1)}, f32[8,128,128]{2,1,0:T(8,128)}, u32[]{:S(2)}) copy-start(f32[8,128,128]{2,1,0:T(8,128)} %convolution_subtract_fusion.5) | copy-start | bytes 1572868
  1295.8 329.5 %collective-permute-start.32 = (f32[8,128]{1,0:T(8,128)S(1)}, f32[8,128]{1,0:T(8,128)S(1)}, u32[]{:S(2)}, u32[]{:S(2)}) collective-permute-start(f32[8,128]{1,0:T(8,128)S(1)} %subtract_subtract_fusion.2), channel_id=1, source_target_pairs={{64,0},{68,4},{72,8},{76,12},{80,16},{84,20},{88,24},{92,28},{96,3... | collective-permute-start | bytes 12296 | tf_op jit(solution)/shard_map/ppermute | solution.py:12
  1297.1 246.4 %collective-permute-start.31 = (f32[8,128]{1,0:T(8,128)S(1)}, f32[8,128]{1,0:T(8,128)S(1)}, u32[]{:S(2)}, u32[]{:S(2)}) collective-permute-start(f32[8,128]{1,0:T(8,128)S(1)} %subtract_subtract_fusion.2), channel_id=1, source_target_pairs={{0,64},{4,68},{8,72},{12,76},{16,80},{20,84},{24,88},{28,92},{32,9... | collective-permute-start | bytes 12296 | tf_op jit(solution)/shard_map/ppermute | solution.py:12
  1424.1 36.4 %collective-permute-start.17 = (f32[8,128,128]{2,1,0:T(8,128)S(1)}, f32[8,128,128]{2,1,0:T(8,128)S(1)}, u32[]{:S(2)}, u32[]{:S(2)}) collective-permute-start(f32[8,128,128]{2,1,0:T(8,128)S(1)} %select_select_fusion.2), channel_id=1, source_target_pairs={{64,0},{68,4},{72,8},{76,12},{80,16},{84,20},{88,24},{92,28},{96,3... | collective-permute-start | bytes 1572872 | tf_op jit(solution)/shard_map/ppermute | solution.py:12
  1425.5 36.5 %collective-permute-start.15 = (f32[8,128,128]{2,1,0:T(8,128)S(1)}, f32[8,128,128]{2,1,0:T(8,128)S(1)}, u32[]{:S(2)}, u32[]{:S(2)}) collective-permute-start(f32[8,128,128]{2,1,0:T(8,128)S(1)} %select_select_fusion.2), channel_id=1, source_target_pairs={{0,64},{4,68},{8,72},{12,76},{16,80},{20,84},{24,88},{28,92},{32,9... | collective-permute-start | bytes 1572872 | tf_op jit(solution)/shard_map/ppermute | solution.py:12
  1452.5 285.9 %collective-permute-start.20 = (f32[8,128,128]{2,1,0:T(8,128)S(1)}, f32[8,128,128]{2,1,0:T(8,128)}, u32[]{:S(2)}, u32[]{:S(2)}) collective-permute-start(f32[8,128,128]{2,1,0:T(8,128)S(1)} %convolution_negate_fusion.3), channel_id=1, source_target_pairs={{0,64},{4,68},{8,72},{12,76},{16,80},{20,84},{24,88},{28,92},{32,9... | collective-permute-start | bytes 1572872 | tf_op jit(solution)/shard_map/ppermute | solution.py:12
  1460.5 286.5 %collective-permute-start.22 = (f32[8,128,128]{2,1,0:T(8,128)}, f32[8,128,128]{2,1,0:T(8,128)}, u32[]{:S(2)}, u32[]{:S(2)}) collective-permute-start(f32[8,128,128]{2,1,0:T(8,128)} %convolution_negate_fusion.2), channel_id=1, source_target_pairs={{64,0},{68,4},{72,8},{76,12},{80,16},{84,20},{88,24},{92,28},{96,3... | collective-permute-start | bytes 1572872 | tf_op jit(solution)/shard_map/ppermute | solution.py:12
  1622.7 10.8 copy-start.3
  1626.5 286.2 %collective-permute-start.34 = (f32[8,128]{1,0:T(8,128)S(1)}, f32[8,128]{1,0:T(8,128)S(1)}, u32[]{:S(2)}, u32[]{:S(2)}) collective-permute-start(f32[8,128]{1,0:T(8,128)S(1)} %subtract_subtract_fusion.1), channel_id=1, source_target_pairs={{128,0},{132,4},{136,8},{140,12},{144,16},{148,20},{152,24},{156,2... | collective-permute-start | bytes 12296 | tf_op jit(solution)/shard_map/ppermute | solution.py:12
  1627.8 204.1 %collective-permute-start.33 = (f32[8,128]{1,0:T(8,128)S(1)}, f32[8,128]{1,0:T(8,128)S(1)}, u32[]{:S(2)}, u32[]{:S(2)}) collective-permute-start(f32[8,128]{1,0:T(8,128)S(1)} %subtract_subtract_fusion.1), channel_id=1, source_target_pairs={{0,128},{4,132},{8,136},{12,140},{16,144},{20,148},{24,152},{28,15... | collective-permute-start | bytes 12296 | tf_op jit(solution)/shard_map/ppermute | solution.py:12
  1737.1 13.1 collective-permute-start.21
  1738.4 11.8 collective-permute-start.19
Sparse Core Ops, SparseCore 0:
  78.1 37.1 reduce-scatter.1
where the time goes:
time: 2140 us; the launch traced here: 2100 us
  other arithmetic  1720 us (80%)
  starting transfers between devices  166 us (8%)
  matrix products  121 us (6%)
  waiting for transfers between devices  39.3 us (2%)
  local copies, waits for them, and re-layouts  32.5 us (2%)
    another operation x18, other arithmetic, lower_solve(): return jax.scipy.linalg.solve_triangular(factor, target, lower=True)  947 us
    another operation x22, other arithmetic, on_device(): factor = jnp.linalg.cholesky(diagonal_block)  669 us
    ppermute x35, starting transfers between devices, passed_along(): return lax.ppermute(array, axis, pairs)  166 us
    another operation x3, other arithmetic, on_device(): jax.scipy.linalg.solve_triangular(factor, forward, lower=True, trans=1)  78.7 us
    another operation x35, matrix products, lower_solve(): return jax.scipy.linalg.solve_triangular(factor, target, lower=True)  44.3 us
  transfers between devices with their start and end apart: 36, of which 3 were waited for; matrix products, arithmetic and copies ran while one was open for 73% of the time, Pallas kernels for 0%

commit v1 on v0

v1 whole, which is shorter than its diff:
```python
import functools

import jax
import jax.numpy as jnp
from jax import lax
from jax.experimental import pallas as pl
from jax.experimental.pallas import tpu as pltpu
from jax.sharding import PartitionSpec as P

F32 = jnp.float32
BF16 = jnp.bfloat16
N = 128
SPAN = 8
MESH = pl.DeviceIdType.MESH


def dot(left, right, dims=((1,), (0,))):
    return lax.dot_general(
        left, right, (dims, ((), ())), precision=lax.Precision.HIGHEST, preferred_element_type=F32
    )


def gram_kernel(rows_ref, label_ref, prec_ref, value_ref, gram_ref, side_ref, left_ref, *, pairs):
    step = pl.program_id(0)
    turned = rows_ref[...].astype(F32).T
    prec = prec_ref[...]
    label = label_ref[...]
    pair = lax.shift_right_logical(label, 1)
    odd = lax.bitwise_and(label, 1)
    scaled = (turned * prec).astype(BF16).astype(F32)
    both = jnp.concatenate(
        [jnp.where(odd == 0, turned, 0.0).astype(BF16), jnp.where(odd == 1, turned, 0.0).astype(BF16)], axis=0
    )
    for p in range(pairs):
        left_ref[pl.ds(p * N, N), :] = jnp.where(pair == p, scaled, 0.0).astype(BF16)
    part = prec * value_ref[...]
    match = lax.broadcasted_iota(jnp.int32, (pairs, part.shape[1]), 0) == pair
    pieces = []
    for _ in range(3):
        top = part.astype(BF16).astype(F32)
        pieces.append(jnp.where(match, top, 0.0).astype(BF16))
        part = part - top
    side = lax.dot_general(
        jnp.concatenate(pieces, axis=0), both, (((1,), (1,)), ((), ())), preferred_element_type=F32
    )
    side = side[:pairs] + side[pairs:2 * pairs] + side[2 * pairs:]

    @pl.when(step == 0)
    def _():
        gram_ref[...] = jnp.zeros_like(gram_ref)
        side_ref[...] = jnp.zeros_like(side_ref)

    side_ref[...] += side
    total = lax.dot_general(
        left_ref[...], both, (((1,), (1,)), ((), ())), preferred_element_type=F32
    )
    for p in range(pairs):
        gram_ref[2 * p] += total[p * N:(p + 1) * N, :N]
        gram_ref[2 * p + 1] += total[p * N:(p + 1) * N, N:]


def tile_terms(rows, label, prec, value, count):
    total_rows = rows.shape[0]
    block = min(1024, total_rows)
    pairs = count // 2
    row = lambda a: a.reshape(1, total_rows)
    flat = pl.BlockSpec((1, block), lambda i: (0, i))
    gram, side = pl.pallas_call(
        functools.partial(gram_kernel, pairs=pairs),
        grid=(total_rows // block,),
        in_specs=[pl.BlockSpec((block, N), lambda i: (i, 0)), flat, flat, flat],
        out_specs=[
            pl.BlockSpec((count, N, N), lambda i: (0, 0, 0)),
            pl.BlockSpec((pairs, 2 * N), lambda i: (0, 0)),
        ],
        out_shape=[
            jax.ShapeDtypeStruct((count, N, N), F32),
            jax.ShapeDtypeStruct((pairs, 2 * N), F32),
        ],
        scratch_shapes=[pltpu.VMEM((pairs * N, block), BF16)],
        compiler_params=pltpu.CompilerParams(vmem_limit_bytes=48 * 2**20),
        name="gram",
    )(rows, row(label), row(prec), row(value))
    return gram, side.reshape(count, N)


def invert(work, batch):
    lane = lax.broadcasted_iota(jnp.int32, (1, N), 1)
    height = lax.broadcasted_iota(jnp.int32, (8, 1), 0)

    def block(_, carry):
        mats = [work[b] for b in range(batch)]
        for j in range(8):
            at = lane == j
            here = height == j
            for b in range(batch):
                m = mats[b]
                row = m[j:j + 1, :]
                scale = 1.0 / row[:, j:j + 1]
                row = jnp.where(at, scale, row * scale)
                column = m[:, j:j + 1]
                m = jnp.where(at, 0.0, m) - column * row
                mats[b] = jnp.concatenate([jnp.where(here, row, m[:8]), m[8:]], axis=0)
        for b in range(batch):
            m = pltpu.roll(mats[b], N - 8, 1)
            work[b] = jnp.concatenate([m[8:], m[:8]], axis=0)
        return carry

    lax.fori_loop(0, N // 8, block, 0)


def pad_rows(row):
    return jnp.broadcast_to(row, (8, N))


def solve_kernel(
    gram_ref, side_ref, kappa_ref, rate_ref, out_ref,
    work, keep, spread2, spread4, held, coupling, send, recv, send_x, recv_x, zs,
    send_sem, recv_sem, x_sems, *, chunks, owner,
):
    me = lax.axis_index("tm")
    chunk, tile = owner.chunk_of(me), owner.tile_of(me)
    levels = chunks.bit_length() - 1
    strides = [2 ** i for i in range(levels)]

    def device(other):
        return (owner.device(other, tile), lax.axis_index("obs"))

    stage_list = []
    for d in sorted(set([1] + strides)):
        stage_list += [-d, d]

    def exists(step):
        return jnp.logical_and(chunk + step >= 0, chunk + step < chunks)

    recv[...] = jnp.zeros_like(recv)
    recv_x[...] = jnp.zeros_like(recv_x)

    barrier = pltpu.get_barrier_semaphore()
    partners = 0
    for step in stage_list:
        @pl.when(exists(step))
        def _():
            pl.semaphore_signal(barrier, inc=1, device_id=device(chunk + step), device_id_type=MESH)
        partners = partners + exists(step).astype(jnp.int32)

    row_id = lax.broadcasted_iota(jnp.int32, (N, N), 0)
    lane_id = lax.broadcasted_iota(jnp.int32, (N, N), 1)
    end = jnp.logical_or(lane_id == 0, lane_id == N - 1)
    degree = jnp.where(end, 1.0, 2.0)
    prior = jnp.where(
        row_id == lane_id, kappa_ref[...] + degree,
        jnp.where(jnp.abs(row_id - lane_id) == 1, -1.0, 0.0),
    )
    weight_row = kappa_ref[...] + degree[:1]
    weight_column = jnp.sum(jnp.where(row_id == lane_id, prior, 0.0), axis=1, keepdims=True)

    def prior_left(m):
        up = jnp.where(row_id == 0, 0.0, pltpu.roll(m, 1, 0))
        down = jnp.where(row_id == N - 1, 0.0, pltpu.roll(m, N - 1, 0))
        return weight_column * m - up - down

    def prior_right(m):
        lanes = lax.broadcasted_iota(jnp.int32, m.shape, 1)
        up = jnp.where(lanes == 0, 0.0, pltpu.roll(m, 1, 1))
        down = jnp.where(lanes == N - 1, 0.0, pltpu.roll(m, N - 1, 1))
        return weight_row * m - up - down

    rates = [rate_ref[i] for i in range(SPAN + 1)]
    first = chunk == 0

    def diagonal(i):
        lead = 1.0
        if i == 0:
            lead = jnp.where(first, 1.0 - rates[0] * rates[0], 1.0)
        g = gram_ref[i]
        return (lead + rates[i + 1] * rates[i + 1]) * prior + 0.5 * (g + g.T)

    def side(i):
        return pad_rows(side_ref[i:i + 1, :])

    for b in range(4):
        work[b] = diagonal(2 * b + 1)
    invert(work, 4)
    sides = {i: side(i) for i in range(0, SPAN, 2)}
    after_side = jnp.zeros((8, N), F32)
    for b in range(4):
        i = 2 * b + 1
        inverse = work[b]
        keep[b] = inverse
        middle = prior_right(prior_left(inverse))
        z = dot(side(i), inverse)
        zs[i] = z
        pz = prior_right(z)
        low, high = rates[i], rates[i + 1]
        held[2 * b] = (diagonal(2 * b) if b == 0 else held[2 * b]) - (low * low) * middle
        coupling[b] = (-low * high) * middle
        sides[i - 1] = sides[i - 1] + low * pz
        if b < 3:
            held[2 * b + 2] = diagonal(2 * b + 2) - (high * high) * middle
            sides[i + 1] = sides[i + 1] + high * pz
        else:
            send[0, 0, 0:N, :] = (high * high) * middle
            after_side = after_side - high * pz

    work[0] = held[2]
    work[1] = held[6]
    invert(work, 2)
    for b, i in ((0, 2), (1, 6)):
        wide = jnp.concatenate([coupling[2 * b], coupling[2 * b + 1]], axis=1)
        tall = jnp.concatenate([coupling[2 * b], coupling[2 * b + 1]], axis=0)
        inverse = work[b]
        x = dot(inverse, wide)
        spread2[b] = x
        z = dot(sides[i], inverse)
        zs[i] = z
        vec = dot(z, wide)
        s = dot(tall, x)
        held[i - 2] = held[i - 2] - s[:N, :N]
        sides[i - 2] = sides[i - 2] - vec[:, :N]
        if b == 0:
            held[4] = held[4] - s[N:, N:]
            sides[4] = sides[4] - vec[:, N:]
            coupling[0] = -s[N:, :N]
            coupling[1] = -s[:N, N:]
        else:
            send[0, 0, 0:N, :] += s[N:, N:]
            after_side = after_side + vec[:, N:]
            coupling[2] = -s[:N, N:]
            coupling[3] = -s[N:, :N]

    work[0] = held[4]
    invert(work, 1)
    wide = jnp.concatenate([coupling[0], coupling[2]], axis=1)
    tall = jnp.concatenate([coupling[1], coupling[3]], axis=0)
    inverse = work[0]
    x = dot(inverse, wide)
    spread4[...] = x
    z = dot(sides[4], inverse)
    zs[4] = z
    vec = dot(z, wide)
    s = dot(tall, x)
    right = -s[:N, N:]
    send[0, 0, 0:N, :] += s[N:, N:]
    send[0, 0, N:2 * N, :] = s[N:, :N]
    send[0, 0, 2 * N:, :] = after_side + vec[:, N:]

    pl.semaphore_wait(barrier, partners)

    def copy(stage, way, step):
        return pltpu.make_async_remote_copy(
            src_ref=send.at[stage, way], dst_ref=recv.at[stage, way],
            send_sem=send_sem.at[stage, way], recv_sem=recv_sem.at[stage, way],
            device_id=device(chunk + step), device_id_type=MESH,
        )

    def start(stage, way, step):
        @pl.when(exists(step))
        def _():
            copy(stage, way, step).start()

    def arrive(stage, way, step):
        @pl.when(exists(-step))
        def _():
            copy(stage, way, step).wait_recv()

    start(0, 0, 1)
    diag = held[0] - s[:N, :N]
    vector = sides[0] - vec[:, :N]
    arrive(0, 0, 1)
    diag = diag - recv[0, 0, 0:N, :]
    left = -recv[0, 0, N:2 * N, :]
    vector = vector - recv[0, 0, 2 * N:, :]

    for stage, stride in enumerate(strides, 1):
        work[0] = diag
        invert(work, 1)
        inverse = work[0]
        wide = jnp.concatenate([left, right], axis=1)
        tall = jnp.concatenate([left.T, right.T], axis=0)
        x = dot(inverse, wide)
        z = dot(vector, inverse)
        vec = dot(z, wide)
        s = dot(tall, x)
        send[stage, 0, 0:N, :] = s[N:, N:]
        send[stage, 0, N:2 * N, :] = s[N:, :N]
        send[stage, 0, 2 * N:, :] = vec[:, N:]
        start(stage, 0, stride)
        send[stage, 1, 0:N, :] = s[:N, :N]
        send[stage, 1, N:2 * N, :] = s[:N, N:]
        send[stage, 1, 2 * N:, :] = vec[:, :N]
        start(stage, 1, -stride)
        arrive(stage, 0, stride)
        arrive(stage, 1, -stride)
        diag = diag - recv[stage, 0, 0:N, :] - recv[stage, 1, 0:N, :]
        left = -recv[stage, 0, N:2 * N, :]
        right = -recv[stage, 1, N:2 * N, :]
        vector = vector - recv[stage, 0, 2 * N:, :] - recv[stage, 1, 2 * N:, :]

    work[0] = diag
    invert(work, 1)
    x0 = dot(vector, work[0])
    send_x[...] = x0

    def copy_x():
        return pltpu.make_async_remote_copy(
            src_ref=send_x, dst_ref=recv_x, send_sem=x_sems.at[0], recv_sem=x_sems.at[1],
            device_id=device(chunk - 1), device_id_type=MESH,
        )

    @pl.when(exists(-1))
    def _():
        copy_x().start()

    @pl.when(exists(1))
    def _():
        copy_x().wait_recv()

    x8 = recv_x[...]
    found = {0: x0, 8: x8}
    last = ((1,), (1,))
    found[4] = zs[4] - dot(jnp.concatenate([x0, x8], axis=1), spread4[...], last)
    for b, i in ((0, 2), (1, 6)):
        found[i] = zs[i] - dot(jnp.concatenate([found[i - 2], found[i + 2]], axis=1), spread2[b], last)
    for b in range(4):
        i = 2 * b + 1
        mixed = rates[i] * found[i - 1] + rates[i + 1] * found[i + 1]
        found[i] = zs[i] + dot(prior_right(mixed), keep[b])
    out_ref[...] = jnp.concatenate([found[i][:1] for i in range(SPAN)], axis=0)

    @pl.when(exists(-1))
    def _():
        copy_x().wait_send()

    @pl.when(exists(1))
    def _():
        copy(0, 0, 1).wait_send()

    for stage, stride in enumerate(strides, 1):
        @pl.when(exists(stride))
        def _():
            copy(stage, 0, stride).wait_send()

        @pl.when(exists(-stride))
        def _():
            copy(stage, 1, -stride).wait_send()


class Consecutive:
    def chunk_of(self, me):
        return me // SPAN

    def tile_of(self, me):
        return me % SPAN

    def device(self, chunk, tile):
        return chunk * SPAN + tile


def solve(gram, side, kappa, rates, chunks):
    stages = chunks.bit_length()
    vmem = pl.BlockSpec(memory_space=pltpu.VMEM)
    return pl.pallas_call(
        functools.partial(solve_kernel, chunks=chunks, owner=Consecutive()),
        in_specs=[vmem, vmem, vmem, pl.BlockSpec(memory_space=pltpu.SMEM)],
        out_specs=vmem,
        out_shape=jax.ShapeDtypeStruct((SPAN, N), F32),
        scratch_shapes=[
            pltpu.VMEM((4, N, N), F32),
            pltpu.VMEM((4, N, N), F32),
            pltpu.VMEM((2, N, 2 * N), F32),
            pltpu.VMEM((N, 2 * N), F32),
            pltpu.VMEM((SPAN, N, N), F32),
            pltpu.VMEM((4, N, N), F32),
            pltpu.VMEM((stages, 2, 2 * N + 8, N), F32),
            pltpu.VMEM((stages, 2, 2 * N + 8, N), F32),
            pltpu.VMEM((8, N), F32),
            pltpu.VMEM((8, N), F32),
            pltpu.VMEM((SPAN, 8, N), F32),
            pltpu.SemaphoreType.DMA((stages, 2)),
            pltpu.SemaphoreType.DMA((stages, 2)),
            pltpu.SemaphoreType.DMA((2,)),
        ],
        compiler_params=pltpu.CompilerParams(
            collective_id=0, has_side_effects=True, vmem_limit_bytes=48 * 2**20
        ),
        name="solve",
    )(gram, side, kappa, rates)


def on_device(weights, tile_of, obs_prec, obs_value, node_kappa, rate):
    owned = node_kappa.shape[0] // N
    peers = lax.axis_size("obs")
    steps = lax.axis_size("tm")
    chunks = steps // SPAN
    me = lax.axis_index("tm")
    all_rates = lax.all_gather(rate[0], "tm")
    gram, side = tile_terms(weights[0], tile_of[0], obs_prec[0], obs_value[0], owned * peers)
    totals = lax.psum_scatter(
        jnp.concatenate([gram, side[:, None, :]], axis=1), "obs", scatter_dimension=0, tiled=True
    )
    groups = [[SPAN * c + k for k in range(SPAN)] for c in range(chunks)]
    mine = lax.all_to_all(totals, "tm", 0, 0, axis_index_groups=groups, tiled=True)
    chunk, tile = me // SPAN, me % SPAN
    kappa = lax.dynamic_slice(node_kappa.reshape(owned, N), (tile, 0), (1, N))
    padded = jnp.concatenate([all_rates, jnp.zeros((SPAN, owned), F32)], axis=0)
    rates = lax.dynamic_slice(padded, (chunk * SPAN, tile), (2 * SPAN, 1))[:, 0]
    states = solve(mine[:, :N], mine[:, N], kappa, rates, chunks)
    back = lax.all_to_all(states, "tm", 0, 0, axis_index_groups=groups, tiled=True)
    return back.reshape(1, owned * N)


def solution(mesh):
    placed = (
        P("tm", "obs", None),
        P("tm", "obs"),
        P("tm", "obs"),
        P("tm", "obs"),
        P("obs"),
        P("tm", "obs"),
    )
    return jax.shard_map(
        on_device, mesh=mesh, in_specs=placed, out_specs=P("tm", "obs"), check_vma=False
    )
```

time: 2140 us -> 263 us (0.12); the launches traced: 2100 us -> 262 us
  other arithmetic: 1720 us -> 1.55 us
  starting transfers between devices: 166 us -> 5.41 us
  Pallas kernels: 0 us -> 133 us
  matrix products: 121 us -> 0 us
  blocking collectives: 0 us -> 67.1 us
  local copies, waits for them, and re-layouts: 32.5 us -> 4.23 us
    another operation x43 -> x0, other arithmetic: 1690 us -> none  [the longest x18 947 us: lower_solve(): return jax.scipy.linalg.solve_triangular(factor, target, lower=True)]
    ppermute x35 -> x0, starting transfers between devices: 166 us -> none  [passed_along(): return lax.ppermute(array, axis, pairs)]
    pallas_call x0 -> x2, Pallas kernels: none -> 133 us  [the longest x1 123 us: solve(): pl.pallas_call(functools.partial(solve_kernel, chunks=chunks, owner=Conse...]
    dot_general x66 -> x0, matrix products: 75.3 us -> none  [the longest x34 34.9 us: pairwise(): jnp.einsum('kab,kac->kbc', left, right, precision=lax.Precision.HIGHEST)]
    all_gather x0 -> x1, blocking collectives: none -> 48.1 us  [on_device(): all_rates = lax.all_gather(rate[0], 'tm')]
    another operation x36 -> x0, matrix products: 45.8 us -> none  [the longest x35 44.3 us: lower_solve(): return jax.scipy.linalg.solve_triangular(factor, target, lower=True)]
  transfers between devices with their start and end apart: 36 -> 2, of which waited for: 3 -> 1; matrix products, arithmetic and copies ran while one was open for 73% -> 0% of each run, Pallas kernels for 0% -> 0%
where the time goes in v1:
time: 263 us; the launch traced here: 262 us
  Pallas kernels  133 us (51%)
  blocking collectives  67.1 us (26%)
  waiting for transfers between devices  37.3 us (14%)
  between operations  13.5 us (5%)
  starting transfers between devices  5.41 us (2%)
  local copies, waits for them, and re-layouts  4.23 us (2%)
    pallas_call x1, Pallas kernels, solve(): pl.pallas_call(functools.partial(solve_kernel, chunks=chunks, owner=Conse...  123 us
    all_gather x1, blocking collectives, on_device(): all_rates = lax.all_gather(rate[0], 'tm')  48.1 us
    reduce_scatter x1, waiting for transfers between devices, on_device(): lax.psum_scatter(jnp.concatenate([gram, side[:, None, :]], axis=1), 'obs'...  37.3 us
    all_to_all x1, blocking collectives, on_device(): lax.all_to_all(states, 'tm', 0, 0, axis_index_groups=groups, tiled=True)  19 us
    pallas_call x1, Pallas kernels, tile_terms(): pl.pallas_call(functools.partial(gram_kernel, pairs=pairs), grid=(total_r...  10.5 us
    all_to_all x1, starting transfers between devices, on_device(): lax.all_to_all(totals, 'tm', 0, 0, axis_index_groups=groups, tiled=True)  5.41 us
  transfers between devices with their start and end apart: 2, of which 1 were waited for; matrix products, arithmetic and copies ran while one was open for 0% of the time, Pallas kernels for 0%

profile of v1, /device:TPU:1, one launch (start us, length us, event | category | flops | bytes accessed | tf_op | source)
XLA Modules:
  0.0 262.4 jit_solution(2641105535909501364)
XLA Ops:
  6.5 0.0 copy-start
  6.5 0.0 reduce-scatter.2.cloned.1.call-start
  6.5 0.0 copy-start.1
  6.5 1.2 copy-done.1
  7.8 0.0 copy-start.2
  7.8 0.7 copy-done.2
  8.5 0.0 copy-start.3
  8.5 0.7 copy-done.3
  9.2 0.0 copy-start.4
  9.2 0.7 copy-done.4
  9.9 10.5 %gram.1 = (f32[32,128,128]{2,1,0:T(8,128)S(1)}, f32[16,256]{1,0:T(8,128)S(1)}) custom-call(bf16[4096,128]{1,0:T(8,128)(2,1)S(1)} %bitcast.13, s32[1,4096]{1,0:T(1,128)S(1)} %copy-done.2, f32[1,4096]{1,0:T(1,128)S(1)} %copy-done.3, f32[1,4096]{1,0:T(1,128)S(1)} %copy-done.4), custom_call_target="tpu_custom_call" | custom-call | tf_op jit(solution)/shard_map/gram/pallas_call | solution.py:68
  20.5 1.5 pad_maximum_fusion
  22.0 0.0 copy-start.5
  22.0 0.0 reduce-scatter.2.cloned.1.call-update
  22.0 37.3 %reduce-scatter.2.cloned.1.call-done = f32[8,129,128]{2,1,0:T(8,128)} async-done(((f32[32,129,128]{2,1,0:T(8,128)}), f32[8,129,128]{2,1,0:T(8,128)}) %reduce-scatter.2.cloned.1.call-update) | async-done | bytes 528400 | tf_op jit(solution)/shard_map/reduce_scatter | solution.py:399
  59.3 5.4 %all-to-all-start = ((f32[8,129,128]{2,1,0:T(8,128)}), f32[8,129,128]{2,1,0:T(8,128)S(1)}, u32[]{:S(2)}, u32[]{:S(2)}) async-start(f32[8,129,128]{2,1,0:T(8,128)} %reduce-scatter.2.cloned.1.call-done), calls=%async_computation.1 | async-start | bytes 1114112 | tf_op jit(solution)/shard_map/all_to_all | solution.py:403
  64.7 0.0 copy-done.5
  64.7 48.1 %all-gather = f32[64,1,8]{2,1,0:T(1,128)S(1)} all-gather(f32[1,1,8]{2,1,0:T(1,128)S(1)} %bitcast.19), channel_id=1, replica_groups=mesh['tm'=64,'obs'=4] {'tm'}, dimensions={0}, use_global_device_ids=true | all-gather | bytes 2080 | tf_op jit(solution)/shard_map/all_gather | solution.py:397
  112.8 0.2 fusion.rate_ref
  113.0 0.0 copy-done
  113.0 0.0 all-to-all-done
  113.1 122.8 %solve.1 = f32[8,128]{1,0:T(8,128)S(1)} custom-call(f32[8,128,128]{2,1,0:T(8,128)S(1)} %slice.8.gram_ref, f32[8,128]{1,0:T(8,128)S(1)} %bitcast.14, f32[1,128]{1,0:T(1,128)S(1)} %constant_dynamic-slice_fusion.kappa_ref, f32[16]{0:T(128)S(1)} %fusion.rate_ref), custom_call_target="tpu_custom_call" | custom-call | tf_op jit(solution)/shard_map/solve/pallas_call | solution.py:363
  235.9 19.0 %all_to_all.14 = f32[8,1,128]{2,1,0:T(1,128)S(1)} all-to-all(f32[8,1,128]{2,1,0:T(1,128)S(1)} %bitcast.15), channel_id=1, replica_groups={{0,4,8,12,16,20,24,28},{32,36,40,44,48,52,56,60},{64,68,72,76,80,84,88,..., dimensions={0} | all-to-all | bytes 8192 | tf_op jit(solution)/shard_map/all_to_all | solution.py:409
  254.9 0.6 copy.16
  (4 shorter events, 0.1 us)
Async XLA Ops:
  6.5 106.5 %copy-start = (f32[1024]{0:T(1024)S(1)}, f32[1024]{0:T(1024)}, u32[]{:S(2)}) copy-start(f32[1024]{0:T(1024)} %param.10) | copy-start | bytes 12292
  6.5 52.8 %reduce-scatter.2.cloned.1.call-start = ((), (), s32[]{:S(2)}) async-start(), calls=%async_computation.3 | async-start | bytes 2785280 | tf_op jit(solution)/shard_map/reduce_scatter | solution.py:399
  6.5 1.2 copy-start.1
  7.8 0.7 copy-start.2
  8.5 0.7 copy-start.3
  9.2 0.7 copy-start.4
  22.0 42.7 %copy-start.5 = (f32[1,8]{1,0:T(1,128)S(1)}, f32[1,8]{1,0:T(1,128)}, u32[]{:S(2)}) copy-start(f32[1,8]{1,0:T(1,128)} %param.11) | copy-start | bytes 100
  59.3 53.7 %all-to-all-start = ((f32[8,129,128]{2,1,0:T(8,128)}), f32[8,129,128]{2,1,0:T(8,128)S(1)}, u32[]{:S(2)}, u32[]{:S(2)}) async-start(f32[8,129,128]{2,1,0:T(8,128)} %reduce-scatter.2.cloned.1.call-done), calls=%async_computation.1 | async-start | bytes 1114112 | tf_op jit(solution)/shard_map/all_to_all | solution.py:403
Sparse Core Ops, SparseCore 0:
  22.2 37.1 reduce-scatter.1

commit v2 on v1

--- a/solution.py
+++ b/solution.py
@@ -84,29 +84,74 @@
     return gram, side.reshape(count, N)
 
 
+def reciprocal(x):
+    r = pltpu.reciprocal(x, approx=True)
+    r = r * (2.0 - x * r)
+    return r * (2.0 - x * r)
+def full(x):
+    return jnp.broadcast_to(x, (8, N))
 def invert(work, batch):
-    lane = lax.broadcasted_iota(jnp.int32, (1, N), 1)
-    height = lax.broadcasted_iota(jnp.int32, (8, 1), 0)
-
-    def block(_, carry):
-        mats = [work[b] for b in range(batch)]
-        for j in range(8):
-            at = lane == j
-            here = height == j
+    panel = 16
+    slabs = panel // 8
+    lane = lax.broadcasted_iota(jnp.int32, (8, N), 1)
+    sub = lax.broadcasted_iota(jnp.int32, (8, N), 0)
+    at = lambda x, s: full(x[s:s + 1, :])
+
+    def load(first, b):
+        return [work[b, pl.ds(pl.multiple_of(first + 8 * v, 8), 8), :] for v in range(slabs)]
+
+    def spread(mats, first):
+        picks = [jnp.full((8, N), k, jnp.int32) + first for k in range(panel)]
+        return [
+            [jnp.take_along_axis(m, pick, axis=1, mode="promise_in_bounds") for m in mats] for pick in picks
+        ]
+
+    def step(index, carry):
+        first = pl.multiple_of(index * panel, panel)
+        rows = [load(first, b) for b in range(batch)]
+        columns = [spread(rows[b], first) for b in range(batch)]
+        place = lane - first
+        for j0 in range(0, panel, 2):
+            j1 = j0 + 1
+            home, s = j0 // 8, j0 % 8
+            pair_lanes = (place == j0) | (place == j1)
+            pair_rows = (sub == s) | (sub == s + 1)
             for b in range(batch):
-                m = mats[b]
-                row = m[j:j + 1, :]
-                scale = 1.0 / row[:, j:j + 1]
-                row = jnp.where(at, scale, row * scale)
-                column = m[:, j:j + 1]
-                m = jnp.where(at, 0.0, m) - column * row
-                mats[b] = jnp.concatenate([jnp.where(here, row, m[:8]), m[8:]], axis=0)
+                e, n = columns[b], rows[b]
+                p, o, q = at(e[j0][home], s), at(e[j0][home], s + 1), at(e[j1][home], s + 1)
+                r = reciprocal(p * q - o * o)
+                w00, w01, w11 = q * r, -(o * r), p * r
+
+                def mix(x0, x1):
+                    return w00 * x0 + w01 * x1, w01 * x0 + w11 * x1
+
+                m0, m1 = list(e[j0]), list(e[j1])
+                m0[home] = jnp.where(sub == s, -1.0, jnp.where(sub == s + 1, 0.0, m0[home]))
+                m1[home] = jnp.where(sub == s, 0.0, jnp.where(sub == s + 1, -1.0, m1[home]))
+                for k in range(j1 + 1, panel):
+                    f0, f1 = mix(at(e[k][home], s), at(e[k][home], s + 1))
+                    for v in range(slabs):
+                        base = jnp.where(pair_rows, 0.0, e[k][v]) if v == home else e[k][v]
+                        e[k][v] = base - (m0[v] * f0 + m1[v] * f1)
+                x0 = jnp.where(pair_lanes, jnp.where(place == j0, 1.0, 0.0), at(n[home], s))
+                x1 = jnp.where(pair_lanes, jnp.where(place == j1, 1.0, 0.0), at(n[home], s + 1))
+                r0, r1 = mix(x0, x1)
+                for v in range(slabs):
+                    gone = (pair_lanes | pair_rows) if v == home else pair_lanes
+                    n[v] = jnp.where(gone, 0.0, n[v]) - (m0[v] * r0 + m1[v] * r1)
+        lane_full = lax.broadcasted_iota(jnp.int32, (N, N), 1) - first
+        row_full = lax.broadcasted_iota(jnp.int32, (N, N), 0) - first
+        in_lanes = (lane_full >= 0) & (lane_full < panel)
+        in_rows = (row_full >= 0) & (row_full < panel)
         for b in range(batch):
-            m = pltpu.roll(mats[b], N - 8, 1)
-            work[b] = jnp.concatenate([m[8:], m[:8]], axis=0)
+            old = work[b]
+            work[b, pl.ds(first, panel), :] = jnp.concatenate(rows[b], axis=0)
+            right = work[b]
+            update = jnp.where(in_lanes, 0.0, old) - dot(jnp.where(in_lanes, old, 0.0), right)
+            work[b] = jnp.where(in_rows, right, update)
         return carry
 
-    lax.fori_loop(0, N // 8, block, 0)
+    lax.fori_loop(0, N // panel, step, 0)
 
 
 def pad_rows(row):

time: 263 us -> 213 us (0.81)
  Pallas kernels: 133 us -> 83.8 us
    pallas_call x1, Pallas kernels: 123 us -> 73.3 us  [solve(): pl.pallas_call(functools.partial(solve_kernel, chunks=chunks, owner=Conse...]
where the time goes in v2:
time: 213 us
  Pallas kernels  83.8 us (39%)
  blocking collectives  67.1 us (32%)
  waiting for transfers between devices  37.3 us (18%)
  between operations  13.5 us (6%)
  starting transfers between devices  5.41 us (3%)
  local copies, waits for them, and re-layouts  4.23 us (2%)
    pallas_call x1, Pallas kernels, solve(): pl.pallas_call(functools.partial(solve_kernel, chunks=chunks, owner=Conse...  73.3 us
    all_gather x1, blocking collectives, on_device(): all_rates = lax.all_gather(rate[0], 'tm')  48.1 us
    reduce_scatter x1, waiting for transfers between devices, on_device(): lax.psum_scatter(jnp.concatenate([gram, side[:, None, :]], axis=1), 'obs'...  37.3 us
    all_to_all x1, blocking collectives, on_device(): lax.all_to_all(states, 'tm', 0, 0, axis_index_groups=groups, tiled=True)  19 us
    pallas_call x1, Pallas kernels, tile_terms(): pl.pallas_call(functools.partial(gram_kernel, pairs=pairs), grid=(total_r...  10.5 us
    all_to_all x1, starting transfers between devices, on_device(): lax.all_to_all(totals, 'tm', 0, 0, axis_index_groups=groups, tiled=True)  5.41 us
  transfers between devices with their start and end apart: 2, of which 1 were waited for; matrix products, arithmetic and copies ran while one was open for 0% of the time, Pallas kernels for 0%

profile of v2, /device:TPU:1, one launch (start us, length us, event | category | flops | bytes accessed | tf_op | source)
XLA Modules:
  0.0 212.9 jit_solution(8197027870452417895)
XLA Ops:
  6.5 0.0 copy-start
  6.5 0.0 reduce-scatter.2.cloned.1.call-start
  6.5 0.0 copy-start.1
  6.5 1.2 copy-done.1
  7.8 0.0 copy-start.2
  7.8 0.7 copy-done.2
  8.5 0.0 copy-start.3
  8.5 0.7 copy-done.3
  9.2 0.0 copy-start.4
  9.2 0.7 copy-done.4
  9.9 10.5 %gram.1 = (f32[32,128,128]{2,1,0:T(8,128)S(1)}, f32[16,256]{1,0:T(8,128)S(1)}) custom-call(bf16[4096,128]{1,0:T(8,128)(2,1)S(1)} %bitcast.13, s32[1,4096]{1,0:T(1,128)S(1)} %copy-done.2, f32[1,4096]{1,0:T(1,128)S(1)} %copy-done.3, f32[1,4096]{1,0:T(1,128)S(1)} %copy-done.4), custom_call_target="tpu_custom_call" | custom-call | tf_op jit(solution)/shard_map/gram/pallas_call | solution.py:68
  20.5 1.5 pad_maximum_fusion
  22.0 0.0 copy-start.5
  22.0 0.0 reduce-scatter.2.cloned.1.call-update
  22.0 37.3 %reduce-scatter.2.cloned.1.call-done = f32[8,129,128]{2,1,0:T(8,128)} async-done(((f32[32,129,128]{2,1,0:T(8,128)}), f32[8,129,128]{2,1,0:T(8,128)}) %reduce-scatter.2.cloned.1.call-update) | async-done | bytes 528400 | tf_op jit(solution)/shard_map/reduce_scatter | solution.py:444
  59.3 5.4 %all-to-all-start = ((f32[8,129,128]{2,1,0:T(8,128)}), f32[8,129,128]{2,1,0:T(8,128)S(1)}, u32[]{:S(2)}, u32[]{:S(2)}) async-start(f32[8,129,128]{2,1,0:T(8,128)} %reduce-scatter.2.cloned.1.call-done), calls=%async_computation.1 | async-start | bytes 1114112 | tf_op jit(solution)/shard_map/all_to_all | solution.py:448
  64.7 0.0 copy-done.5
  64.7 48.1 %all-gather = f32[64,1,8]{2,1,0:T(1,128)S(1)} all-gather(f32[1,1,8]{2,1,0:T(1,128)S(1)} %bitcast.19), channel_id=1, replica_groups=mesh['tm'=64,'obs'=4] {'tm'}, dimensions={0}, use_global_device_ids=true | all-gather | bytes 2080 | tf_op jit(solution)/shard_map/all_gather | solution.py:442
  112.8 0.2 fusion.rate_ref
  113.0 0.0 copy-done
  113.0 0.0 all-to-all-done
  113.1 73.3 %solve.1 = f32[8,128]{1,0:T(8,128)S(1)} custom-call(f32[8,128,128]{2,1,0:T(8,128)S(1)} %slice.8.gram_ref, f32[8,128]{1,0:T(8,128)S(1)} %bitcast.14, f32[1,128]{1,0:T(1,128)S(1)} %constant_dynamic-slice_fusion.kappa_ref, f32[16]{0:T(128)S(1)} %fusion.rate_ref), custom_call_target="tpu_custom_call" | custom-call | tf_op jit(solution)/shard_map/solve/pallas_call | solution.py:408
  186.4 19.0 %all_to_all.14 = f32[8,1,128]{2,1,0:T(1,128)S(1)} all-to-all(f32[8,1,128]{2,1,0:T(1,128)S(1)} %bitcast.15), channel_id=1, replica_groups={{0,4,8,12,16,20,24,28},{32,36,40,44,48,52,56,60},{64,68,72,76,80,84,88,..., dimensions={0} | all-to-all | bytes 8192 | tf_op jit(solution)/shard_map/all_to_all | solution.py:454
  205.4 0.6 copy.16
  (4 shorter events, 0.1 us)
Async XLA Ops:
  6.5 106.5 %copy-start = (f32[1024]{0:T(1024)S(1)}, f32[1024]{0:T(1024)}, u32[]{:S(2)}) copy-start(f32[1024]{0:T(1024)} %param.10) | copy-start | bytes 12292
  6.5 52.8 %reduce-scatter.2.cloned.1.call-start = ((), (), s32[]{:S(2)}) async-start(), calls=%async_computation.3 | async-start | bytes 2785280 | tf_op jit(solution)/shard_map/reduce_scatter | solution.py:444
  6.5 1.2 copy-start.1
  7.8 0.7 copy-start.2
  8.5 0.7 copy-start.3
  9.2 0.7 copy-start.4
  22.0 42.7 %copy-start.5 = (f32[1,8]{1,0:T(1,128)S(1)}, f32[1,8]{1,0:T(1,128)}, u32[]{:S(2)}) copy-start(f32[1,8]{1,0:T(1,128)} %param.11) | copy-start | bytes 100
  59.3 53.7 %all-to-all-start = ((f32[8,129,128]{2,1,0:T(8,128)}), f32[8,129,128]{2,1,0:T(8,128)S(1)}, u32[]{:S(2)}, u32[]{:S(2)}) async-start(f32[8,129,128]{2,1,0:T(8,128)} %reduce-scatter.2.cloned.1.call-done), calls=%async_computation.1 | async-start | bytes 1114112 | tf_op jit(solution)/shard_map/all_to_all | solution.py:448
Sparse Core Ops, SparseCore 0:
  22.2 37.1 reduce-scatter.1

commit v3 on v2

--- a/solution.py
+++ b/solution.py
@@ -20,68 +20,270 @@
     )
 
 
-def gram_kernel(rows_ref, label_ref, prec_ref, value_ref, gram_ref, side_ref, left_ref, *, pairs):
-    step = pl.program_id(0)
-    turned = rows_ref[...].astype(F32).T
-    prec = prec_ref[...]
-    label = label_ref[...]
-    pair = lax.shift_right_logical(label, 1)
-    odd = lax.bitwise_and(label, 1)
-    scaled = (turned * prec).astype(BF16).astype(F32)
-    both = jnp.concatenate(
-        [jnp.where(odd == 0, turned, 0.0).astype(BF16), jnp.where(odd == 1, turned, 0.0).astype(BF16)], axis=0
+class Owner:
+    def chunk_of(self, me):
+        return 2 * (me // 16) + me % 2
+
+    def tile_of(self, me):
+        return (me % 16) // 2
+
+    def device(self, chunk, tile):
+        return 16 * (chunk // 2) + 2 * tile + chunk % 2
+
+
+OWNER = Owner()
+FOLD = N // 2 + 8
+DIAG, SIDE, RATE = N // 2, N // 2 + 1, N // 2 + 2
+
+
+def fold(block, side):
+    half = N // 2
+    both = block + block.T
+    row = lax.broadcasted_iota(jnp.int32, (half, N), 0)
+    lane = lax.broadcasted_iota(jnp.int32, (half, N), 1) - half
+    low = both[half:]
+    packed = jnp.where((lane >= 0) & (lane <= row), pltpu.roll(both[:half], half, 1), low)
+    diag = jnp.sum(jnp.where(lane == row, low, 0.0), axis=0, keepdims=True)
+    sub = lax.broadcasted_iota(jnp.int32, (8, N), 0)
+    extra = jnp.where(sub == 0, diag, jnp.where(sub == 1, side, 0.0))
+    return jnp.concatenate([packed, extra], axis=0)
+
+
+def unfold(packed):
+    half = N // 2
+    rows = packed[:half]
+    turned = pltpu.roll(rows, half, 1)
+    row = lax.broadcasted_iota(jnp.int32, (half, N), 0)
+    lane = lax.broadcasted_iota(jnp.int32, (half, N), 1)
+    top = jnp.where(lane < row, 0.5 * turned, jnp.where(lane == row, 0.25 * turned, 0.0))
+    far = lane - half
+    low = jnp.where(
+        (far < 0) | (far > row), 0.5 * rows, jnp.where(far == row, 0.25 * packed[half:half + 1], 0.0)
     )
-    for p in range(pairs):
-        left_ref[pl.ds(p * N, N), :] = jnp.where(pair == p, scaled, 0.0).astype(BF16)
-    part = prec * value_ref[...]
-    match = lax.broadcasted_iota(jnp.int32, (pairs, part.shape[1]), 0) == pair
+    both = jnp.concatenate([top, low], axis=0)
+    return both + both.T
+
+
+def front_kernel(
+    rows_ref, label_ref, prec_ref, value_ref, rate_ref, out_ref, next_ref,
+    scaled, paired, left, sides, send1, recv1, own, send2, recv2, send3, recv3,
+    send1_sem, recv1_sem, send2_sem, recv2_sem, send3_sem, recv3_sem,
+    *, chunks, peers,
+):
+    me, x = lax.axis_index("tm"), lax.axis_index("obs")
+    plus, minus = lax.rem(x + 1, peers), lax.rem(x + peers - 1, peers)
+    far = lax.rem(x + 2, peers)
+    chunk, slot = me // SPAN, me % SPAN
+    my_chunk, my_tile = OWNER.chunk_of(me), OWNER.tile_of(me)
+    total_rows = rows_ref.shape[0]
+    block = min(1024, total_rows)
+    pairs = sides.shape[0]
+    tell = jnp.logical_and(slot == 0, chunk > 0)
+    told = my_chunk < chunks - 1
+
+    barrier = pltpu.get_barrier_semaphore()
+    awaited = 2
+    for other in (plus, minus):
+        pl.semaphore_signal(barrier, inc=1, device_id=(me, other), device_id_type=MESH)
+    for i in range(SPAN):
+        source = my_chunk * SPAN + i
+
+        @pl.when(source != me)
+        def _():
+            pl.semaphore_signal(barrier, inc=1, device_id=(source, x), device_id_type=MESH)
+
+        awaited = awaited + (OWNER.device(chunk, i) != me).astype(jnp.int32)
+        awaited = awaited + jnp.logical_and(tell, OWNER.device(chunk - 1, i) != me).astype(jnp.int32)
+    teller = (my_chunk + 1) * SPAN
+
+    @pl.when(jnp.logical_and(told, teller != me))
+    def _():
+        pl.semaphore_signal(barrier, inc=1, device_id=(teller, x), device_id_type=MESH)
+
+    pair = lax.shift_right_logical(label_ref[...], 1)
+    odd = lax.bitwise_and(label_ref[...], 1)
+    ones = lambda mask: jnp.where(mask, 1.0, 0.0).astype(BF16)
+    for step in range(total_rows // block):
+        here = slice(step * block, (step + 1) * block)
+        turned = rows_ref[here, :].astype(F32).T
+        scaled[:, here] = (turned * prec_ref[:, here]).astype(BF16)
+        turned = turned.astype(BF16)
+        paired[:N, here] = turned * ones(odd[:, here] == 0)
+        paired[N:, here] = turned * ones(odd[:, here] == 1)
+    last = (((1,), (1,)), ((), ()))
+    part = prec_ref[...] * value_ref[...]
+    match = lax.broadcasted_iota(jnp.int32, (pairs, total_rows), 0) == pair
     pieces = []
     for _ in range(3):
         top = part.astype(BF16).astype(F32)
         pieces.append(jnp.where(match, top, 0.0).astype(BF16))
         part = part - top
     side = lax.dot_general(
-        jnp.concatenate(pieces, axis=0), both, (((1,), (1,)), ((), ())), preferred_element_type=F32
+        jnp.concatenate(pieces, axis=0), paired[...], last, preferred_element_type=F32
     )
-    side = side[:pairs] + side[pairs:2 * pairs] + side[2 * pairs:]
-
-    @pl.when(step == 0)
-    def _():
-        gram_ref[...] = jnp.zeros_like(gram_ref)
-        side_ref[...] = jnp.zeros_like(side_ref)
-
-    side_ref[...] += side
-    total = lax.dot_general(
-        left_ref[...], both, (((1,), (1,)), ((), ())), preferred_element_type=F32
-    )
-    for p in range(pairs):
-        gram_ref[2 * p] += total[p * N:(p + 1) * N, :N]
-        gram_ref[2 * p + 1] += total[p * N:(p + 1) * N, N:]
-
-
-def tile_terms(rows, label, prec, value, count):
+    sides[...] = side[:pairs] + side[pairs:2 * pairs] + side[2 * pairs:]
+
+    def copy1(way, stage):
+        return pltpu.make_async_remote_copy(
+            src_ref=send1.at[way, stage], dst_ref=recv1.at[way, stage],
+            send_sem=send1_sem.at[way, stage], recv_sem=recv1_sem.at[way, stage],
+            device_id=(me, plus if way == 0 else minus), device_id_type=MESH,
+        )
+
+    def half(group, part, target, added=()):
+        first = 4 * group + 2 * part
+        for p in range(2):
+            left[p * N:(p + 1) * N, :] = scaled[...] * ones(pair == first + p)
+        total = lax.dot_general(left[...], paired[...], last, preferred_element_type=F32)
+        for p in range(2):
+            side_row = sides[pl.ds(first + p, 1), :]
+            for o in range(2):
+                q = 2 * p + o
+                value = fold(
+                    total[p * N:(p + 1) * N, o * N:(o + 1) * N], side_row[:, o * N:(o + 1) * N]
+                )
+                for way, stage in added:
+                    value = value + recv1[way, stage, q]
+                target[q] = value
+
+    half(far, 0, send1.at[0, 0])
+    half(far, 1, send1.at[1, 0])
+    pl.semaphore_wait(barrier, awaited)
+    copy1(0, 0).start()
+    copy1(1, 0).start()
+
+    def copy3(k):
+        return pltpu.make_async_remote_copy(
+            src_ref=send3.at[k], dst_ref=recv3, send_sem=send3_sem.at[k], recv_sem=recv3_sem.at[0],
+            device_id=(OWNER.device(chunk - 1, k), x), device_id_type=MESH,
+        )
+
+    recv3_is_own = jnp.logical_and(told, teller == me)
+
+    @pl.when(jnp.logical_not(told))
+    def _():
+        recv3[...] = jnp.zeros_like(recv3)
+
+    @pl.when(tell)
+    def _():
+        for k in range(SPAN):
+            send3[k] = full(rate_ref[:, k:k + 1])
+
+            @pl.when(OWNER.device(chunk - 1, k) != me)
+            def _():
+                copy3(k).start()
+
+    @pl.when(recv3_is_own)
+    def _():
+        recv3[...] = send3[my_tile]
+
+    half(plus, 1, send1.at[0, 1])
+    copy1(0, 1).start()
+    half(minus, 0, send1.at[1, 1])
+    copy1(1, 1).start()
+    copy1(0, 0).wait_recv()
+    half(plus, 0, send1.at[0, 2], [(0, 0)])
+    copy1(0, 2).start()
+    copy1(1, 0).wait_recv()
+    half(minus, 1, send1.at[1, 2], [(1, 0)])
+    copy1(1, 2).start()
+    half(x, 0, own.at[0])
+    half(x, 1, own.at[1])
+
+    sub = lax.broadcasted_iota(jnp.int32, (8, N), 0)
+
+    def copy2(k):
+        return pltpu.make_async_remote_copy(
+            src_ref=send2.at[k], dst_ref=recv2.at[slot],
+            send_sem=send2_sem.at[k], recv_sem=recv2_sem.at[slot],
+            device_id=(OWNER.device(chunk, k), x), device_id_type=MESH,
+        )
+
+    def arrival(i):
+        return pltpu.make_async_remote_copy(
+            src_ref=send2.at[0], dst_ref=recv2.at[i], send_sem=send2_sem.at[0], recv_sem=recv2_sem.at[i],
+            device_id=(me, plus), device_id_type=MESH,
+        )
+
+    for part in range(2):
+        copy1(part, 2).wait_recv()
+        copy1(1 - part, 1).wait_recv()
+        for q in range(4):
+            k = 4 * part + q
+            value = own[part, q] + recv1[part, 2, q] + recv1[1 - part, 1, q]
+            send2[k, :N // 2] = value[:N // 2]
+            send2[k, N // 2:] = jnp.where(sub == 2, full(rate_ref[:, k:k + 1]), value[N // 2:])
+            mine = OWNER.device(chunk, k) == me
+
+            @pl.when(jnp.logical_not(mine))
+            def _():
+                copy2(k).start()
+
+            @pl.when(mine)
+            def _():
+                recv2[slot] = send2[k]
+
+    for i in range(SPAN):
+        @pl.when(my_chunk * SPAN + i != me)
+        def _():
+            arrival(i).wait_recv()
+
+        out_ref[i] = recv2[i]
+
+    @pl.when(jnp.logical_and(told, teller != me))
+    def _():
+        copy3(0).wait_recv()
+
+    next_ref[...] = recv3[...]
+    for way in range(2):
+        for stage in range(3):
+            copy1(way, stage).wait_send()
+    for k in range(SPAN):
+        @pl.when(OWNER.device(chunk, k) != me)
+        def _():
+            copy2(k).wait_send()
+
+        @pl.when(jnp.logical_and(tell, OWNER.device(chunk - 1, k) != me))
+        def _():
+            copy3(k).wait_send()
+
+
+def front(rows, label, prec, value, rate, chunks, peers):
     total_rows = rows.shape[0]
-    block = min(1024, total_rows)
-    pairs = count // 2
     row = lambda a: a.reshape(1, total_rows)
-    flat = pl.BlockSpec((1, block), lambda i: (0, i))
-    gram, side = pl.pallas_call(
-        functools.partial(gram_kernel, pairs=pairs),
-        grid=(total_rows // block,),
-        in_specs=[pl.BlockSpec((block, N), lambda i: (i, 0)), flat, flat, flat],
-        out_specs=[
-            pl.BlockSpec((count, N, N), lambda i: (0, 0, 0)),
-            pl.BlockSpec((pairs, 2 * N), lambda i: (0, 0)),
+    vmem = pl.BlockSpec(memory_space=pltpu.VMEM)
+    return pl.pallas_call(
+        functools.partial(front_kernel, chunks=chunks, peers=peers),
+        in_specs=[vmem] * 5,
+        out_specs=[vmem, vmem],
+        out_shape=[
+            jax.ShapeDtypeStruct((SPAN, FOLD, N), F32),
+            jax.ShapeDtypeStruct((8, N), F32),
         ],
-        out_shape=[
-            jax.ShapeDtypeStruct((count, N, N), F32),
-            jax.ShapeDtypeStruct((pairs, 2 * N), F32),
+        scratch_shapes=[
+            pltpu.VMEM((N, total_rows), BF16),
+            pltpu.VMEM((2 * N, total_rows), BF16),
+            pltpu.VMEM((2 * N, total_rows), BF16),
+            pltpu.VMEM((4 * peers, 2 * N), F32),
+            pltpu.VMEM((2, 3, 4, FOLD, N), F32),
+            pltpu.VMEM((2, 3, 4, FOLD, N), F32),
+            pltpu.VMEM((2, 4, FOLD, N), F32),
+            pltpu.VMEM((SPAN, FOLD, N), F32),
+            pltpu.VMEM((SPAN, FOLD, N), F32),
+            pltpu.VMEM((SPAN, 8, N), F32),
+            pltpu.VMEM((8, N), F32),
+            pltpu.SemaphoreType.DMA((2, 3)),
+            pltpu.SemaphoreType.DMA((2, 3)),
+            pltpu.SemaphoreType.DMA((SPAN,)),
+            pltpu.SemaphoreType.DMA((SPAN,)),
+            pltpu.SemaphoreType.DMA((SPAN,)),
+            pltpu.SemaphoreType.DMA((1,)),
         ],
-        scratch_shapes=[pltpu.VMEM((pairs * N, block), BF16)],
-        compiler_params=pltpu.CompilerParams(vmem_limit_bytes=48 * 2**20),
-        name="gram",
-    )(rows, row(label), row(prec), row(value))
-    return gram, side.reshape(count, N)
+        compiler_params=pltpu.CompilerParams(
+            collective_id=1, has_side_effects=True, vmem_limit_bytes=48 * 2**20
+        ),
+        name="front",
+    )(rows, row(label), row(prec), row(value), rate)
 
 
 def reciprocal(x):
@@ -159,17 +361,18 @@
 
 
 def solve_kernel(
-    gram_ref, side_ref, kappa_ref, rate_ref, out_ref,
-    work, keep, spread2, spread4, held, coupling, send, recv, send_x, recv_x, zs,
-    send_sem, recv_sem, x_sems, *, chunks, owner,
+    packed_ref, next_ref, kappa_ref, out_ref,
+    work, keep, spread2, spread4, held, coupling, send, recv, send_x, recv_x, zs, send_out, recv_out,
+    send_sem, recv_sem, x_sems, send_out_sem, recv_out_sem, *, chunks,
 ):
     me = lax.axis_index("tm")
-    chunk, tile = owner.chunk_of(me), owner.tile_of(me)
+    chunk, tile = OWNER.chunk_of(me), OWNER.tile_of(me)
+    home, place = me // SPAN, me % SPAN
     levels = chunks.bit_length() - 1
     strides = [2 ** i for i in range(levels)]
 
     def device(other):
-        return (owner.device(other, tile), lax.axis_index("obs"))
+        return (OWNER.device(other, tile), lax.axis_index("obs"))
 
     stage_list = []
     for d in sorted(set([1] + strides)):
@@ -188,6 +391,13 @@
         def _():
             pl.semaphore_signal(barrier, inc=1, device_id=device(chunk + step), device_id_type=MESH)
         partners = partners + exists(step).astype(jnp.int32)
+    for i in range(SPAN):
+        @pl.when(OWNER.device(home, i) != me)
+        def _():
+            pl.semaphore_signal(
+                barrier, inc=1, device_id=(OWNER.device(home, i), lax.axis_index("obs")), device_id_type=MESH
+            )
+        partners = partners + (chunk * SPAN + i != me).astype(jnp.int32)
 
     row_id = lax.broadcasted_iota(jnp.int32, (N, N), 0)
     lane_id = lax.broadcasted_iota(jnp.int32, (N, N), 1)
@@ -211,18 +421,17 @@
         down = jnp.where(lanes == N - 1, 0.0, pltpu.roll(m, N - 1, 1))
         return weight_row * m - up - down
 
-    rates = [rate_ref[i] for i in range(SPAN + 1)]
+    rates = [packed_ref[i, RATE:RATE + 1, :] for i in range(SPAN)] + [next_ref[:1]]
     first = chunk == 0
 
     def diagonal(i):
         lead = 1.0
         if i == 0:
             lead = jnp.where(first, 1.0 - rates[0] * rates[0], 1.0)
-        g = gram_ref[i]
-        return (lead + rates[i + 1] * rates[i + 1]) * prior + 0.5 * (g + g.T)
+        return (lead + rates[i + 1] * rates[i + 1]) * prior + unfold(packed_ref[i])
 
     def side(i):
-        return pad_rows(side_ref[i:i + 1, :])
+        return pad_rows(packed_ref[i, SIDE:SIDE + 1, :])
 
     for b in range(4):
         work[b] = diagonal(2 * b + 1)
@@ -371,7 +580,42 @@
         i = 2 * b + 1
         mixed = rates[i] * found[i - 1] + rates[i + 1] * found[i + 1]
         found[i] = zs[i] + dot(prior_right(mixed), keep[b])
-    out_ref[...] = jnp.concatenate([found[i][:1] for i in range(SPAN)], axis=0)
+    def copy_out(i):
+        return pltpu.make_async_remote_copy(
+            src_ref=send_out.at[i], dst_ref=recv_out.at[tile],
+            send_sem=send_out_sem.at[i], recv_sem=recv_out_sem.at[tile],
+            device_id=(chunk * SPAN + i, lax.axis_index("obs")), device_id_type=MESH,
+        )
+
+    def arrive_out(k):
+        return pltpu.make_async_remote_copy(
+            src_ref=send_out.at[0], dst_ref=recv_out.at[k],
+            send_sem=send_out_sem.at[0], recv_sem=recv_out_sem.at[k],
+            device_id=(OWNER.device(home, k), lax.axis_index("obs")), device_id_type=MESH,
+        )
+
+    for i in range(SPAN):
+        send_out[i] = found[i]
+
+        @pl.when(chunk * SPAN + i != me)
+        def _():
+            copy_out(i).start()
+
+        @pl.when(chunk * SPAN + i == me)
+        def _():
+            recv_out[tile] = send_out[i]
+
+    for k in range(SPAN):
+        @pl.when(OWNER.device(home, k) != me)
+        def _():
+            arrive_out(k).wait_recv()
+
+        out_ref[:, k * N:(k + 1) * N] = recv_out[k, :1, :]
+
+    for i in range(SPAN):
+        @pl.when(chunk * SPAN + i != me)
+        def _():
+            copy_out(i).wait_send()
 
     @pl.when(exists(-1))
     def _():
@@ -391,25 +635,14 @@
             copy(stage, 1, -stride).wait_send()
 
 
-class Consecutive:
-    def chunk_of(self, me):
-        return me // SPAN
-
-    def tile_of(self, me):
-        return me % SPAN
-
-    def device(self, chunk, tile):
-        return chunk * SPAN + tile
-
-
-def solve(gram, side, kappa, rates, chunks):
+def solve(packed, after, kappa, chunks):
     stages = chunks.bit_length()
     vmem = pl.BlockSpec(memory_space=pltpu.VMEM)
     return pl.pallas_call(
-        functools.partial(solve_kernel, chunks=chunks, owner=Consecutive()),
-        in_specs=[vmem, vmem, vmem, pl.BlockSpec(memory_space=pltpu.SMEM)],
+        functools.partial(solve_kernel, chunks=chunks),
+        in_specs=[vmem] * 3,
         out_specs=vmem,
-        out_shape=jax.ShapeDtypeStruct((SPAN, N), F32),
+        out_shape=jax.ShapeDtypeStruct((1, SPAN * N), F32),
         scratch_shapes=[
             pltpu.VMEM((4, N, N), F32),
             pltpu.VMEM((4, N, N), F32),
@@ -422,37 +655,30 @@
             pltpu.VMEM((8, N), F32),
             pltpu.VMEM((8, N), F32),
             pltpu.VMEM((SPAN, 8, N), F32),
+            pltpu.VMEM((SPAN, 8, N), F32),
+            pltpu.VMEM((SPAN, 8, N), F32),
             pltpu.SemaphoreType.DMA((stages, 2)),
             pltpu.SemaphoreType.DMA((stages, 2)),
             pltpu.SemaphoreType.DMA((2,)),
+            pltpu.SemaphoreType.DMA((SPAN,)),
+            pltpu.SemaphoreType.DMA((SPAN,)),
         ],
         compiler_params=pltpu.CompilerParams(
             collective_id=0, has_side_effects=True, vmem_limit_bytes=48 * 2**20
         ),
         name="solve",
-    )(gram, side, kappa, rates)
+    )(packed, after, kappa)
 
 
 def on_device(weights, tile_of, obs_prec, obs_value, node_kappa, rate):
     owned = node_kappa.shape[0] // N
-    peers = lax.axis_size("obs")
-    steps = lax.axis_size("tm")
-    chunks = steps // SPAN
-    me = lax.axis_index("tm")
-    all_rates = lax.all_gather(rate[0], "tm")
-    gram, side = tile_terms(weights[0], tile_of[0], obs_prec[0], obs_value[0], owned * peers)
-    totals = lax.psum_scatter(
-        jnp.concatenate([gram, side[:, None, :]], axis=1), "obs", scatter_dimension=0, tiled=True
+    chunks = lax.axis_size("tm") // SPAN
+    tile = OWNER.tile_of(lax.axis_index("tm"))
+    packed, after = front(
+        weights[0], tile_of[0], obs_prec[0], obs_value[0], rate, chunks, lax.axis_size("obs")
     )
-    groups = [[SPAN * c + k for k in range(SPAN)] for c in range(chunks)]
-    mine = lax.all_to_all(totals, "tm", 0, 0, axis_index_groups=groups, tiled=True)
-    chunk, tile = me // SPAN, me % SPAN
     kappa = lax.dynamic_slice(node_kappa.reshape(owned, N), (tile, 0), (1, N))
-    padded = jnp.concatenate([all_rates, jnp.zeros((SPAN, owned), F32)], axis=0)
-    rates = lax.dynamic_slice(padded, (chunk * SPAN, tile), (2 * SPAN, 1))[:, 0]
-    states = solve(mine[:, :N], mine[:, N], kappa, rates, chunks)
-    back = lax.all_to_all(states, "tm", 0, 0, axis_index_groups=groups, tiled=True)
-    return back.reshape(1, owned * N)
+    return solve(packed, after, kappa, chunks)
 
 
 def solution(mesh):

time: 213 us -> 99.8 us (0.47)
  blocking collectives: 67.1 us -> 0 us
  waiting for transfers between devices: 37.3 us -> 0 us
  between operations: 13.5 us -> 0.05 us
  Pallas kernels: 83.8 us -> 96.5 us
  starting transfers between devices: 5.41 us -> 0 us
    all_gather x1 -> x0, blocking collectives: 48.1 us -> none  [on_device(): all_rates = lax.all_gather(rate[0], 'tm')]
    reduce_scatter x1 -> x0, waiting for transfers between devices: 37.3 us -> none  [on_device(): lax.psum_scatter(jnp.concatenate([gram, side[:, None, :]], axis=1), 'obs'...]
    all_to_all x1 -> x0, blocking collectives: 19 us -> none  [on_device(): lax.all_to_all(states, 'tm', 0, 0, axis_index_groups=groups, tiled=True)]
    pallas_call x2, Pallas kernels: 83.8 us -> 96.5 us  [the longest x1 69.6 us: solve(): pl.pallas_call(functools.partial(solve_kernel, chunks=chunks), in_specs=[...]
    all_to_all x1 -> x0, starting transfers between devices: 5.41 us -> none  [on_device(): lax.all_to_all(totals, 'tm', 0, 0, axis_index_groups=groups, tiled=True)]
  transfers between devices with their start and end apart: 2 -> 0, of which waited for: 1 -> 0; matrix products, arithmetic and copies ran while one was open for 0% -> 0% of each run, Pallas kernels for 0% -> 0%
where the time goes in v3:
time: 99.8 us; the launch traced here: 99.6 us
  Pallas kernels  96.5 us (97%)
  local copies, waits for them, and re-layouts  3.14 us (3%)
    pallas_call x1, Pallas kernels, solve(): pl.pallas_call(functools.partial(solve_kernel, chunks=chunks), in_specs=[...  69.6 us
    pallas_call x1, Pallas kernels, front(): pl.pallas_call(functools.partial(front_kernel, chunks=chunks, peers=peers...  26.9 us
    unnamed x13, local copies, waits for them, and re-layouts  3.13 us

profile of v3, /device:TPU:1, one launch (start us, length us, event | category | flops | bytes accessed | tf_op | source)
XLA Modules:
  0.0 99.6 jit_solution(656458849271306481)
XLA Ops:
  0.0 0.0 copy-start
  0.0 0.0 copy-start.4
  0.0 0.0 copy-start.2
  0.0 0.0 copy-start.3
  0.0 0.6 copy-done
  0.7 0.0 copy-start.5
  0.7 0.0 copy-done.4
  0.7 0.0 copy-done.2
  0.8 0.0 copy-done.3
  0.8 0.6 copy-done.5
  1.4 0.0 copy-start.1
  1.4 1.2 %copy-done.1 = bf16[1,4096,128]{2,1,0:T(8,128)(2,1)S(1)} copy-done((bf16[1,4096,128]{2,1,0:T(8,128)(2,1)S(1)}, bf16[1,4096,128]{2,1,0:T(8,128)(2,1)}, u32[]{:S(2)}) %copy-start.1) | copy-done | bytes 1048600
  2.6 26.9 %front.1 = (f32[8,72,128]{2,1,0:T(8,128)S(1)}, f32[8,128]{1,0:T(8,128)S(1)}) custom-call(bf16[4096,128]{1,0:T(8,128)(2,1)S(1)} %bitcast.3, s32[1,4096]{1,0:T(1,128)S(1)} %copy-done.2, f32[1,4096]{1,0:T(1,128)S(1)} %copy-done.3, f32[1,4096]{1,0:T(1,128)S(1)} %copy-done.4, f32[1,8]{1,0:T(1,128)S(1)} %copy-done.5), custom_call_target="tpu_custom_call" | custom-call | tf_op jit(solution)/shard_map/front/pallas_call | solution.py:255
  29.5 69.6 %solve.1 = f32[1,1024]{1,0:T(1,128)S(1)} custom-call(f32[8,72,128]{2,1,0:T(8,128)S(1)} %get-tuple-element.7.packed_ref, f32[8,128]{1,0:T(8,128)S(1)} %get-tuple-element.8.next_ref, f32[1,128]{1,0:T(1,128)S(1)} %constant_dynamic-slice_fusion.kappa_ref), custom_call_target="tpu_custom_call" | custom-call | tf_op jit(solution)/shard_map/solve/pallas_call | solution.py:641
  99.1 0.6 copy.8
  (1 shorter events, 0.0 us)
Async XLA Ops:
  0.0 0.7 copy-start
  0.0 0.7 copy-start.4
  0.0 0.7 copy-start.2
  0.0 0.8 copy-start.3
  0.7 0.7 copy-start.5
  1.4 1.2 %copy-start.1 = (bf16[1,4096,128]{2,1,0:T(8,128)(2,1)S(1)}, bf16[1,4096,128]{2,1,0:T(8,128)(2,1)}, u32[]{:S(2)}) copy-start(bf16[1,4096,128]{2,1,0:T(8,128)(2,1)} %param.6) | copy-start | bytes 3145732

commit v4 on v3

--- a/solution.py
+++ b/solution.py
@@ -64,10 +64,11 @@
     return both + both.T
 
 
-def front_kernel(
-    rows_ref, label_ref, prec_ref, value_ref, rate_ref, out_ref, next_ref,
+def front_part(
+    rows_hbm, label_hbm, prec_hbm, value_hbm, rate_hbm, kappa_hbm,
+    rows_ref, label_ref, prec_ref, value_ref, rate_ref, kappa_ref,
     scaled, paired, left, sides, send1, recv1, own, send2, recv2, send3, recv3,
-    send1_sem, recv1_sem, send2_sem, recv2_sem, send3_sem, recv3_sem,
+    load_sem, send1_sem, recv1_sem, send2_sem, recv2_sem, send3_sem, recv3_sem,
     *, chunks, peers,
 ):
     me, x = lax.axis_index("tm"), lax.axis_index("obs")
@@ -78,6 +79,23 @@
     total_rows = rows_ref.shape[0]
     block = min(1024, total_rows)
     pairs = sides.shape[0]
+    loads = [
+        pltpu.make_async_copy(source, target, load_sem.at[i])
+        for i, (source, target) in enumerate(
+            (
+                (label_hbm, label_ref), (prec_hbm, prec_ref), (value_hbm, value_ref),
+                (rate_hbm, rate_ref), (kappa_hbm, kappa_ref),
+            )
+        )
+    ]
+    row_loads = [
+        pltpu.make_async_copy(
+            rows_hbm.at[0, pl.ds(i * block, block)], rows_ref.at[pl.ds(i * block, block)], load_sem.at[len(loads) + i]
+        )
+        for i in range(total_rows // block)
+    ]
+    for load in loads + row_loads:
+        load.start()
     tell = jnp.logical_and(slot == 0, chunk > 0)
     told = my_chunk < chunks - 1
 
@@ -100,11 +118,34 @@
     def _():
         pl.semaphore_signal(barrier, inc=1, device_id=(teller, x), device_id_type=MESH)
 
+    for stride in [2 ** i for i in range(max(1, chunks.bit_length() - 1))]:
+        for other in (my_chunk - stride, my_chunk + stride):
+            exists = jnp.logical_and(other >= 0, other < chunks)
+
+            @pl.when(exists)
+            def _():
+                pl.semaphore_signal(
+                    barrier, inc=1, device_id=(OWNER.device(other, my_tile), x), device_id_type=MESH
+                )
+
+            awaited = awaited + exists.astype(jnp.int32)
+    for i in range(SPAN):
+        source = OWNER.device(chunk, i)
+
+        @pl.when(source != me)
+        def _():
+            pl.semaphore_signal(barrier, inc=1, device_id=(source, x), device_id_type=MESH)
+
+        awaited = awaited + (my_chunk * SPAN + i != me).astype(jnp.int32)
+
+    for load in loads:
+        load.wait()
     pair = lax.shift_right_logical(label_ref[...], 1)
     odd = lax.bitwise_and(label_ref[...], 1)
     ones = lambda mask: jnp.where(mask, 1.0, 0.0).astype(BF16)
     for step in range(total_rows // block):
         here = slice(step * block, (step + 1) * block)
+        row_loads[step].wait()
         turned = rows_ref[here, :].astype(F32).T
         scaled[:, here] = (turned * prec_ref[:, here]).astype(BF16)
         turned = turned.astype(BF16)
@@ -123,10 +164,12 @@
     )
     sides[...] = side[:pairs] + side[pairs:2 * pairs] + side[2 * pairs:]
 
-    def copy1(way, stage):
+    def copy1(way, stage, q=None):
+        piece = (way, stage) if q is None else (way, stage, q)
+        sem = stage + (q or 0)
         return pltpu.make_async_remote_copy(
-            src_ref=send1.at[way, stage], dst_ref=recv1.at[way, stage],
-            send_sem=send1_sem.at[way, stage], recv_sem=recv1_sem.at[way, stage],
+            src_ref=send1.at[piece], dst_ref=recv1.at[piece],
+            send_sem=send1_sem.at[way, sem], recv_sem=recv1_sem.at[way, sem],
             device_id=(me, plus if way == 0 else minus), device_id_type=MESH,
         )
 
@@ -183,10 +226,12 @@
     copy1(1, 1).start()
     copy1(0, 0).wait_recv()
     half(plus, 0, send1.at[0, 2], [(0, 0)])
-    copy1(0, 2).start()
+    for q in range(4):
+        copy1(0, 2, q).start()
     copy1(1, 0).wait_recv()
     half(minus, 1, send1.at[1, 2], [(1, 0)])
-    copy1(1, 2).start()
+    for q in range(4):
+        copy1(1, 2, q).start()
     half(x, 0, own.at[0])
     half(x, 1, own.at[1])
 
@@ -205,10 +250,11 @@
             device_id=(me, plus), device_id_type=MESH,
         )
 
-    for part in range(2):
-        copy1(part, 2).wait_recv()
-        copy1(1 - part, 1).wait_recv()
-        for q in range(4):
+    copy1(0, 1).wait_recv()
+    copy1(1, 1).wait_recv()
+    for q in range(4):
+        for part in range(2):
+            copy1(part, 2, q).wait_recv()
             k = 4 * part + q
             value = own[part, q] + recv1[part, 2, q] + recv1[1 - part, 1, q]
             send2[k, :N // 2] = value[:N // 2]
@@ -228,75 +274,49 @@
         def _():
             arrival(i).wait_recv()
 
-        out_ref[i] = recv2[i]
-
     @pl.when(jnp.logical_and(told, teller != me))
     def _():
         copy3(0).wait_recv()
 
-    next_ref[...] = recv3[...]
-    for way in range(2):
-        for stage in range(3):
-            copy1(way, stage).wait_send()
-    for k in range(SPAN):
-        @pl.when(OWNER.device(chunk, k) != me)
-        def _():
-            copy2(k).wait_send()
-
-        @pl.when(jnp.logical_and(tell, OWNER.device(chunk - 1, k) != me))
-        def _():
-            copy3(k).wait_send()
-
-
-def front(rows, label, prec, value, rate, chunks, peers):
-    total_rows = rows.shape[0]
-    row = lambda a: a.reshape(1, total_rows)
-    vmem = pl.BlockSpec(memory_space=pltpu.VMEM)
-    return pl.pallas_call(
-        functools.partial(front_kernel, chunks=chunks, peers=peers),
-        in_specs=[vmem] * 5,
-        out_specs=[vmem, vmem],
-        out_shape=[
-            jax.ShapeDtypeStruct((SPAN, FOLD, N), F32),
-            jax.ShapeDtypeStruct((8, N), F32),
-        ],
-        scratch_shapes=[
-            pltpu.VMEM((N, total_rows), BF16),
-            pltpu.VMEM((2 * N, total_rows), BF16),
-            pltpu.VMEM((2 * N, total_rows), BF16),
-            pltpu.VMEM((4 * peers, 2 * N), F32),
-            pltpu.VMEM((2, 3, 4, FOLD, N), F32),
-            pltpu.VMEM((2, 3, 4, FOLD, N), F32),
-            pltpu.VMEM((2, 4, FOLD, N), F32),
-            pltpu.VMEM((SPAN, FOLD, N), F32),
-            pltpu.VMEM((SPAN, FOLD, N), F32),
-            pltpu.VMEM((SPAN, 8, N), F32),
-            pltpu.VMEM((8, N), F32),
-            pltpu.SemaphoreType.DMA((2, 3)),
-            pltpu.SemaphoreType.DMA((2, 3)),
-            pltpu.SemaphoreType.DMA((SPAN,)),
-            pltpu.SemaphoreType.DMA((SPAN,)),
-            pltpu.SemaphoreType.DMA((SPAN,)),
-            pltpu.SemaphoreType.DMA((1,)),
-        ],
-        compiler_params=pltpu.CompilerParams(
-            collective_id=1, has_side_effects=True, vmem_limit_bytes=48 * 2**20
-        ),
-        name="front",
-    )(rows, row(label), row(prec), row(value), rate)
+    def finish():
+        for way in range(2):
+            copy1(way, 0).wait_send()
+            copy1(way, 1).wait_send()
+            for q in range(4):
+                copy1(way, 2, q).wait_send()
+        for k in range(SPAN):
+            @pl.when(OWNER.device(chunk, k) != me)
+            def _():
+                copy2(k).wait_send()
+
+            @pl.when(jnp.logical_and(tell, OWNER.device(chunk - 1, k) != me))
+            def _():
+                copy3(k).wait_send()
+
+    return finish
 
 
 def reciprocal(x):
     r = pltpu.reciprocal(x, approx=True)
     r = r * (2.0 - x * r)
     return r * (2.0 - x * r)
+
 def full(x):
     return jnp.broadcast_to(x, (8, N))
-def invert(work, batch):
-    panel = 16
+
+def tree_sum(parts):
+    while len(parts) > 1:
+        parts = [parts[x] + parts[x + 1] for x in range(0, len(parts), 2)]
+    return parts[0]
+
+
+def invert(work, batch, panel=16):
+    unroll = 2 if batch <= 2 else 1
     slabs = panel // 8
     lane = lax.broadcasted_iota(jnp.int32, (8, N), 1)
     sub = lax.broadcasted_iota(jnp.int32, (8, N), 0)
+    lane_full = lax.broadcasted_iota(jnp.int32, (N, N), 1)
+    row_full = lax.broadcasted_iota(jnp.int32, (N, N), 0)
     at = lambda x, s: full(x[s:s + 1, :])
 
     def load(first, b):
@@ -304,15 +324,26 @@
 
     def spread(mats, first):
         picks = [jnp.full((8, N), k, jnp.int32) + first for k in range(panel)]
-        return [
-            [jnp.take_along_axis(m, pick, axis=1, mode="promise_in_bounds") for m in mats] for pick in picks
-        ]
+        return [[jnp.take_along_axis(m, pick, axis=1, mode="promise_in_bounds") for m in mats] for pick in picks]
+
+    def update(first, b):
+        in_lanes = (lane_full >= first) & (lane_full < first + panel)
+        in_rows = (row_full >= first) & (row_full < first + panel)
+        old = work[b]
+        change = dot(jnp.where(in_lanes & ~in_rows, old, 0.0), old)
+        return jnp.where(in_lanes & ~in_rows, 0.0, old) - change
 
     def step(index, carry):
         first = pl.multiple_of(index * panel, panel)
-        rows = [load(first, b) for b in range(batch)]
+        after = pl.multiple_of(lax.rem(first + panel, N), panel)
+        rows = [[carry[b * slabs + v] for v in range(slabs)] for b in range(batch)]
         columns = [spread(rows[b], first) for b in range(batch)]
         place = lane - first
+        inside = (place >= 0) & (place < panel)
+        for b in range(batch):
+            work[b] = update(first - panel, b)
+        coming = [load(after, b) for b in range(batch)]
+        below = [spread(coming[b], first) for b in range(batch)]
         for j0 in range(0, panel, 2):
             j1 = j0 + 1
             home, s = j0 // 8, j0 % 8
@@ -341,26 +372,30 @@
                 for v in range(slabs):
                     gone = (pair_lanes | pair_rows) if v == home else pair_lanes
                     n[v] = jnp.where(gone, 0.0, n[v]) - (m0[v] * r0 + m1[v] * r1)
-        lane_full = lax.broadcasted_iota(jnp.int32, (N, N), 1) - first
-        row_full = lax.broadcasted_iota(jnp.int32, (N, N), 0) - first
-        in_lanes = (lane_full >= 0) & (lane_full < panel)
-        in_rows = (row_full >= 0) & (row_full < panel)
+        out = []
         for b in range(batch):
-            old = work[b]
             work[b, pl.ds(first, panel), :] = jnp.concatenate(rows[b], axis=0)
-            right = work[b]
-            update = jnp.where(in_lanes, 0.0, old) - dot(jnp.where(in_lanes, old, 0.0), right)
-            work[b] = jnp.where(in_rows, right, update)
+            out += [
+                jnp.where(inside, 0.0, coming[b][v])
+                - tree_sum([below[b][k][v] * at(rows[b][k // 8], k % 8) for k in range(panel)])
+                for v in range(slabs)
+            ]
+        return tuple(out)
+
+    def steps(index, carry):
+        for i in range(unroll):
+            carry = step(index * unroll + i, carry)
         return carry
-
-    lax.fori_loop(0, N // panel, step, 0)
+    lax.fori_loop(0, N // panel // unroll, steps, tuple(m for b in range(batch) for m in load(0, b)))
+    for b in range(batch):
+        work[b] = update(N - panel, b)
 
 
 def pad_rows(row):
     return jnp.broadcast_to(row, (8, N))
 
 
-def solve_kernel(
+def solve_part(
     packed_ref, next_ref, kappa_ref, out_ref,
     work, keep, spread2, spread4, held, coupling, send, recv, send_x, recv_x, zs, send_out, recv_out,
     send_sem, recv_sem, x_sems, send_out_sem, recv_out_sem, *, chunks,
@@ -374,40 +409,19 @@
     def device(other):
         return (OWNER.device(other, tile), lax.axis_index("obs"))
 
-    stage_list = []
-    for d in sorted(set([1] + strides)):
-        stage_list += [-d, d]
-
     def exists(step):
         return jnp.logical_and(chunk + step >= 0, chunk + step < chunks)
 
-    recv[...] = jnp.zeros_like(recv)
-    recv_x[...] = jnp.zeros_like(recv_x)
-
-    barrier = pltpu.get_barrier_semaphore()
-    partners = 0
-    for step in stage_list:
-        @pl.when(exists(step))
-        def _():
-            pl.semaphore_signal(barrier, inc=1, device_id=device(chunk + step), device_id_type=MESH)
-        partners = partners + exists(step).astype(jnp.int32)
-    for i in range(SPAN):
-        @pl.when(OWNER.device(home, i) != me)
-        def _():
-            pl.semaphore_signal(
-                barrier, inc=1, device_id=(OWNER.device(home, i), lax.axis_index("obs")), device_id_type=MESH
-            )
-        partners = partners + (chunk * SPAN + i != me).astype(jnp.int32)
-
+    kappa = kappa_ref[pl.ds(tile, 1), :]
     row_id = lax.broadcasted_iota(jnp.int32, (N, N), 0)
     lane_id = lax.broadcasted_iota(jnp.int32, (N, N), 1)
     end = jnp.logical_or(lane_id == 0, lane_id == N - 1)
     degree = jnp.where(end, 1.0, 2.0)
     prior = jnp.where(
-        row_id == lane_id, kappa_ref[...] + degree,
+        row_id == lane_id, kappa + degree,
         jnp.where(jnp.abs(row_id - lane_id) == 1, -1.0, 0.0),
     )
-    weight_row = kappa_ref[...] + degree[:1]
+    weight_row = kappa + degree[:1]
     weight_column = jnp.sum(jnp.where(row_id == lane_id, prior, 0.0), axis=1, keepdims=True)
 
     def prior_left(m):
@@ -496,60 +510,70 @@
     s = dot(tall, x)
     right = -s[:N, N:]
     send[0, 0, 0:N, :] += s[N:, N:]
-    send[0, 0, N:2 * N, :] = s[N:, :N]
-    send[0, 0, 2 * N:, :] = after_side + vec[:, N:]
-
-    pl.semaphore_wait(barrier, partners)
-
-    def copy(stage, way, step):
+    send[0, 0, N + 8:, :] = s[N:, :N]
+    send[0, 0, N:N + 8, :] = after_side + vec[:, N:]
+
+    now, later = pl.ds(0, N + 8), pl.ds(N + 8, N)
+    last_stage = len(strides)
+
+    def copy(stage, way, step, part):
+        rows = later if part else now
         return pltpu.make_async_remote_copy(
-            src_ref=send.at[stage, way], dst_ref=recv.at[stage, way],
-            send_sem=send_sem.at[stage, way], recv_sem=recv_sem.at[stage, way],
+            src_ref=send.at[stage, way, rows], dst_ref=recv.at[stage, way, rows],
+            send_sem=send_sem.at[stage, way, part], recv_sem=recv_sem.at[stage, way, part],
             device_id=device(chunk + step), device_id_type=MESH,
         )
 
-    def start(stage, way, step):
+    def start(stage, way, step, part):
         @pl.when(exists(step))
         def _():
-            copy(stage, way, step).start()
-
-    def arrive(stage, way, step):
+            copy(stage, way, step, part).start()
+
+    def arrive(stage, way, step, part):
         @pl.when(exists(-step))
         def _():
-            copy(stage, way, step).wait_recv()
-
-    start(0, 0, 1)
+            copy(stage, way, step, part).wait_recv()
+
+    start(0, 0, 1, 0)
+    start(0, 0, 1, 1)
     diag = held[0] - s[:N, :N]
     vector = sides[0] - vec[:, :N]
-    arrive(0, 0, 1)
+    arrive(0, 0, 1, 0)
     diag = diag - recv[0, 0, 0:N, :]
-    left = -recv[0, 0, N:2 * N, :]
-    vector = vector - recv[0, 0, 2 * N:, :]
+    vector = vector - recv[0, 0, N:N + 8, :]
 
     for stage, stride in enumerate(strides, 1):
         work[0] = diag
         invert(work, 1)
         inverse = work[0]
+        z = dot(vector, inverse)
+        if stage == 1:
+            arrive(0, 0, 1, 1)
+        else:
+            arrive(stage - 1, 0, stride // 2, 1)
+            arrive(stage - 1, 1, -(stride // 2), 1)
+            right = -recv[stage - 1, 1, N + 8:, :]
+        left = -recv[stage - 1, 0, N + 8:, :]
         wide = jnp.concatenate([left, right], axis=1)
         tall = jnp.concatenate([left.T, right.T], axis=0)
         x = dot(inverse, wide)
-        z = dot(vector, inverse)
         vec = dot(z, wide)
         s = dot(tall, x)
         send[stage, 0, 0:N, :] = s[N:, N:]
-        send[stage, 0, N:2 * N, :] = s[N:, :N]
-        send[stage, 0, 2 * N:, :] = vec[:, N:]
-        start(stage, 0, stride)
+        send[stage, 0, N:N + 8, :] = vec[:, N:]
+        start(stage, 0, stride, 0)
         send[stage, 1, 0:N, :] = s[:N, :N]
-        send[stage, 1, N:2 * N, :] = s[:N, N:]
-        send[stage, 1, 2 * N:, :] = vec[:, :N]
-        start(stage, 1, -stride)
-        arrive(stage, 0, stride)
-        arrive(stage, 1, -stride)
+        send[stage, 1, N:N + 8, :] = vec[:, :N]
+        start(stage, 1, -stride, 0)
+        if stage < last_stage:
+            send[stage, 0, N + 8:, :] = s[N:, :N]
+            start(stage, 0, stride, 1)
+            send[stage, 1, N + 8:, :] = s[:N, N:]
+            start(stage, 1, -stride, 1)
+        arrive(stage, 0, stride, 0)
+        arrive(stage, 1, -stride, 0)
         diag = diag - recv[stage, 0, 0:N, :] - recv[stage, 1, 0:N, :]
-        left = -recv[stage, 0, N:2 * N, :]
-        right = -recv[stage, 1, N:2 * N, :]
-        vector = vector - recv[stage, 0, 2 * N:, :] - recv[stage, 1, 2 * N:, :]
+        vector = vector - recv[stage, 0, N:N + 8, :] - recv[stage, 1, N:N + 8, :]
 
     work[0] = diag
     invert(work, 1)
@@ -621,64 +645,106 @@
     def _():
         copy_x().wait_send()
 
-    @pl.when(exists(1))
-    def _():
-        copy(0, 0, 1).wait_send()
-
-    for stage, stride in enumerate(strides, 1):
-        @pl.when(exists(stride))
-        def _():
-            copy(stage, 0, stride).wait_send()
-
-        @pl.when(exists(-stride))
-        def _():
-            copy(stage, 1, -stride).wait_send()
-
-
-def solve(packed, after, kappa, chunks):
+    for part in range(2):
+        @pl.when(exists(1))
+        def _():
+            copy(0, 0, 1, part).wait_send()
+
+        for stage, stride in enumerate(strides, 1):
+            if part == 0 or stage < last_stage:
+                @pl.when(exists(stride))
+                def _():
+                    copy(stage, 0, stride, part).wait_send()
+
+                @pl.when(exists(-stride))
+                def _():
+                    copy(stage, 1, -stride, part).wait_send()
+
+
+def whole_kernel(
+    rows_hbm, label_hbm, prec_hbm, value_hbm, rate_hbm, kappa_hbm, out_ref, *scratch, chunks, peers, parts
+):
+    for slots in (scratch[parts + 7], scratch[parts + 9]):
+        slots[...] = jnp.zeros_like(slots)
+    finish = front_part(
+        rows_hbm, label_hbm, prec_hbm, value_hbm, rate_hbm, kappa_hbm, *scratch[:parts],
+        chunks=chunks, peers=peers,
+    )
+    kappa, packed, after = scratch[5], scratch[14], scratch[16]
+    solve_part(packed, after, kappa, out_ref, *scratch[parts:], chunks=chunks)
+    finish()
+
+
+def posterior(rows, label, prec, value, rate, kappa, chunks, peers):
+    total_rows = rows.shape[1]
     stages = chunks.bit_length()
     vmem = pl.BlockSpec(memory_space=pltpu.VMEM)
+    hbm = pl.BlockSpec(memory_space=pltpu.HBM)
+    dma = pltpu.SemaphoreType.DMA
+    front_scratch = [
+        pltpu.VMEM((total_rows, N), BF16),
+        pltpu.VMEM((1, total_rows), jnp.int32),
+        pltpu.VMEM((1, total_rows), F32),
+        pltpu.VMEM((1, total_rows), F32),
+        pltpu.VMEM(rate.shape, F32),
+        pltpu.VMEM(kappa.shape, F32),
+        pltpu.VMEM((N, total_rows), BF16),
+        pltpu.VMEM((2 * N, total_rows), BF16),
+        pltpu.VMEM((2 * N, total_rows), BF16),
+        pltpu.VMEM((4 * peers, 2 * N), F32),
+        pltpu.VMEM((2, 3, 4, FOLD, N), F32),
+        pltpu.VMEM((2, 3, 4, FOLD, N), F32),
+        pltpu.VMEM((2, 4, FOLD, N), F32),
+        pltpu.VMEM((SPAN, FOLD, N), F32),
+        pltpu.VMEM((SPAN, FOLD, N), F32),
+        pltpu.VMEM((SPAN, 8, N), F32),
+        pltpu.VMEM((8, N), F32),
+        dma((5 + total_rows // min(1024, total_rows),)),
+        dma((2, 6)),
+        dma((2, 6)),
+        dma((SPAN,)),
+        dma((SPAN,)),
+        dma((SPAN,)),
+        dma((1,)),
+    ]
+    solve_scratch = [
+        pltpu.VMEM((4, N, N), F32),
+        pltpu.VMEM((4, N, N), F32),
+        pltpu.VMEM((2, N, 2 * N), F32),
+        pltpu.VMEM((N, 2 * N), F32),
+        pltpu.VMEM((SPAN, N, N), F32),
+        pltpu.VMEM((4, N, N), F32),
+        pltpu.VMEM((stages, 2, 2 * N + 8, N), F32),
+        pltpu.VMEM((stages, 2, 2 * N + 8, N), F32),
+        pltpu.VMEM((8, N), F32),
+        pltpu.VMEM((8, N), F32),
+        pltpu.VMEM((SPAN, 8, N), F32),
+        pltpu.VMEM((SPAN, 8, N), F32),
+        pltpu.VMEM((SPAN, 8, N), F32),
+        dma((stages, 2, 2)),
+        dma((stages, 2, 2)),
+        dma((2,)),
+        dma((SPAN,)),
+        dma((SPAN,)),
+    ]
     return pl.pallas_call(
-        functools.partial(solve_kernel, chunks=chunks),
-        in_specs=[vmem] * 3,
+        functools.partial(whole_kernel, chunks=chunks, peers=peers, parts=len(front_scratch)),
+        in_specs=[hbm] * 6,
         out_specs=vmem,
         out_shape=jax.ShapeDtypeStruct((1, SPAN * N), F32),
-        scratch_shapes=[
-            pltpu.VMEM((4, N, N), F32),
-            pltpu.VMEM((4, N, N), F32),
-            pltpu.VMEM((2, N, 2 * N), F32),
-            pltpu.VMEM((N, 2 * N), F32),
-            pltpu.VMEM((SPAN, N, N), F32),
-            pltpu.VMEM((4, N, N), F32),
-            pltpu.VMEM((stages, 2, 2 * N + 8, N), F32),
-            pltpu.VMEM((stages, 2, 2 * N + 8, N), F32),
-            pltpu.VMEM((8, N), F32),
-            pltpu.VMEM((8, N), F32),
-            pltpu.VMEM((SPAN, 8, N), F32),
-            pltpu.VMEM((SPAN, 8, N), F32),
-            pltpu.VMEM((SPAN, 8, N), F32),
-            pltpu.SemaphoreType.DMA((stages, 2)),
-            pltpu.SemaphoreType.DMA((stages, 2)),
-            pltpu.SemaphoreType.DMA((2,)),
-            pltpu.SemaphoreType.DMA((SPAN,)),
-            pltpu.SemaphoreType.DMA((SPAN,)),
-        ],
+        scratch_shapes=front_scratch + solve_scratch,
         compiler_params=pltpu.CompilerParams(
-            collective_id=0, has_side_effects=True, vmem_limit_bytes=48 * 2**20
+            collective_id=0, has_side_effects=True, vmem_limit_bytes=64 * 2**20 - 2**16
         ),
-        name="solve",
-    )(packed, after, kappa)
+        name="posterior",
+    )(rows, label, prec, value, rate, kappa)
 
 
 def on_device(weights, tile_of, obs_prec, obs_value, node_kappa, rate):
-    owned = node_kappa.shape[0] // N
-    chunks = lax.axis_size("tm") // SPAN
-    tile = OWNER.tile_of(lax.axis_index("tm"))
-    packed, after = front(
-        weights[0], tile_of[0], obs_prec[0], obs_value[0], rate, chunks, lax.axis_size("obs")
+    return posterior(
+        weights, tile_of, obs_prec, obs_value, rate, node_kappa.reshape(-1, N),
+        lax.axis_size("tm") // SPAN, lax.axis_size("obs"),
     )
-    kappa = lax.dynamic_slice(node_kappa.reshape(owned, N), (tile, 0), (1, N))
-    return solve(packed, after, kappa, chunks)
 
 
 def solution(mesh):

time: 99.8 us -> 87 us (0.87)
  Pallas kernels: 96.5 us -> 85.5 us
  local copies, waits for them, and re-layouts: 3.14 us -> 1.28 us
    pallas_call x2 -> x1, Pallas kernels: 96.5 us -> 85.5 us  [posterior(): pl.pallas_call(functools.partial(whole_kernel, chunks=chunks, peers=peers...]
    unnamed x13 -> x1, local copies, waits for them, and re-layouts: 3.13 us -> 1.28 us
where the time goes in v4:
time: 87 us; the launch traced here: 86.8 us
  Pallas kernels  85.5 us (98%)
  local copies, waits for them, and re-layouts  1.28 us (1%)
    pallas_call x1, Pallas kernels, posterior(): pl.pallas_call(functools.partial(whole_kernel, chunks=chunks, peers=peers...  85.5 us

profile of v4, /device:TPU:1, one launch (start us, length us, event | category | flops | bytes accessed | tf_op | source)
XLA Modules:
  0.0 86.8 jit_solution(13078747146554462601)
XLA Ops:
  0.0 85.5 %posterior.1 = f32[1,1024]{1,0:T(1,128)} custom-call(bf16[1,4096,128]{2,1,0:T(8,128)(2,1)} %rows_hbm.1, s32[1,4096]{1,0:T(1,128)} %label_hbm.1, f32[1,4096]{1,0:T(1,128)} %prec_hbm.1, f32[1,4096]{1,0:T(1,128)} %value_hbm.1, f32[1,8]{1,0:T(1,128)} %rate_hbm.1, f32[8,128]{1,0:T(8,128)} %bitcast.1), custom_call_target="tpu_custom_call" | custom-call | tf_op jit(solution)/shard_map/posterior/pallas_call | solution.py:730
  85.5 1.3 %copy.8 = f32[1,1024]{1,0:T(1,128)} copy(f32[1,1024]{1,0:T(1,128)} %posterior.1) | data formatting | bytes 8192

commit v5 on v4

--- a/solution.py
+++ b/solution.py
@@ -298,7 +298,6 @@
 
 def reciprocal(x):
     r = pltpu.reciprocal(x, approx=True)
-    r = r * (2.0 - x * r)
     return r * (2.0 - x * r)
 
 def full(x):
@@ -355,23 +354,21 @@
                 r = reciprocal(p * q - o * o)
                 w00, w01, w11 = q * r, -(o * r), p * r
 
-                def mix(x0, x1):
-                    return w00 * x0 + w01 * x1, w01 * x0 + w11 * x1
-
                 m0, m1 = list(e[j0]), list(e[j1])
                 m0[home] = jnp.where(sub == s, -1.0, jnp.where(sub == s + 1, 0.0, m0[home]))
                 m1[home] = jnp.where(sub == s, 0.0, jnp.where(sub == s + 1, -1.0, m1[home]))
+                g0 = [m0[v] * w00 + m1[v] * w01 for v in range(slabs)]
+                g1 = [m0[v] * w01 + m1[v] * w11 for v in range(slabs)]
                 for k in range(j1 + 1, panel):
-                    f0, f1 = mix(at(e[k][home], s), at(e[k][home], s + 1))
+                    f0, f1 = at(e[k][home], s), at(e[k][home], s + 1)
                     for v in range(slabs):
                         base = jnp.where(pair_rows, 0.0, e[k][v]) if v == home else e[k][v]
-                        e[k][v] = base - (m0[v] * f0 + m1[v] * f1)
+                        e[k][v] = base - (g0[v] * f0 + g1[v] * f1)
                 x0 = jnp.where(pair_lanes, jnp.where(place == j0, 1.0, 0.0), at(n[home], s))
                 x1 = jnp.where(pair_lanes, jnp.where(place == j1, 1.0, 0.0), at(n[home], s + 1))
-                r0, r1 = mix(x0, x1)
                 for v in range(slabs):
                     gone = (pair_lanes | pair_rows) if v == home else pair_lanes
-                    n[v] = jnp.where(gone, 0.0, n[v]) - (m0[v] * r0 + m1[v] * r1)
+                    n[v] = jnp.where(gone, 0.0, n[v]) - (g0[v] * x0 + g1[v] * x1)
         out = []
         for b in range(batch):
             work[b, pl.ds(first, panel), :] = jnp.concatenate(rows[b], axis=0)

time: 87 us -> 84.4 us (0.970)
  Pallas kernels: 85.5 us -> 82.9 us
    pallas_call x1, Pallas kernels: 85.5 us -> 82.9 us  [posterior(): pl.pallas_call(functools.partial(whole_kernel, chunks=chunks, peers=peers...]
where the time goes in v5:
time: 84.4 us; the launch traced here: 84.1 us
  Pallas kernels  82.9 us (98%)
  local copies, waits for them, and re-layouts  1.28 us (2%)
    pallas_call x1, Pallas kernels, posterior(): pl.pallas_call(functools.partial(whole_kernel, chunks=chunks, peers=peers...  82.9 us

profile of v5, /device:TPU:1, one launch (start us, length us, event | category | flops | bytes accessed | tf_op | source)
XLA Modules:
  0.0 84.1 jit_solution(6116467409763830072)
XLA Ops:
  0.0 82.9 %posterior.1 = f32[1,1024]{1,0:T(1,128)} custom-call(bf16[1,4096,128]{2,1,0:T(8,128)(2,1)} %rows_hbm.1, s32[1,4096]{1,0:T(1,128)} %label_hbm.1, f32[1,4096]{1,0:T(1,128)} %prec_hbm.1, f32[1,4096]{1,0:T(1,128)} %value_hbm.1, f32[1,8]{1,0:T(1,128)} %rate_hbm.1, f32[8,128]{1,0:T(8,128)} %bitcast.1), custom_call_target="tpu_custom_call" | custom-call | tf_op jit(solution)/shard_map/posterior/pallas_call | solution.py:727
  82.9 1.3 %copy.8 = f32[1,1024]{1,0:T(1,128)} copy(f32[1,1024]{1,0:T(1,128)} %posterior.1) | data formatting | bytes 8192
